TPU v7x, 256 devices: a whole 4x4x8 slice. The times are simulated.
256 devices in a mesh: rep: 16 (over y, x), con: 16 (over z, core).
Axes of the slice: x: 4, y: 4, z: 8, core: 2. Of those that a mesh axis runs over, the one named last changes fastest.
Arguments:
- audio_hidden: bfloat16 [40960, 1280], P(('rep', 'con')), may hold values from -6 to 6
- score_hidden: bfloat16 [40960, 1280], P(('rep', 'con')), may hold values from -6 to 6
- audio_proj: bfloat16 [40960, 1024], P(('rep', 'con')), may hold values from -300 to 300
- score_proj: bfloat16 [40960, 1024], P(('rep', 'con')), may hold values from -300 to 300
- labels: int32 [16, 2560], P('rep', 'con'), may hold values from 0 to 2559, as said below
- q_seed: float32 [1024, 64], replicated, may hold values from -6 to 6
- err_audio: float32 [16, 1280, 1024], P('rep', 'con'), may hold values from -4 to 4
- err_score: float32 [16, 1280, 1024], P('rep', 'con'), may hold values from -4 to 4
Outputs:
- p_audio: float32 [1280, 64], P('con')
- q_audio: float32 [1024, 64], replicated
- new_err_audio: float32 [16, 1280, 1024], P('rep', 'con')
- p_score: float32 [1280, 64], P('con')
- q_score: float32 [1024, 64], replicated
- new_err_score: float32 [16, 1280, 1024], P('rep', 'con')
Inputs may be any that keep to these rules, and one draw needn't show every extreme that they name: Each row of labels is a permutation of 0 to 2559: audio row i of replica r pairs with score row labels[r, i] of the same replica.
All inputs are finite; a program needn't handle non-finite values.
Results may differ from a plain program's by a relative error of at most 0.00057.
Values may be sent and summed in bfloat16 or wider, within the bound.
A program may use at most 64 MiB of HBM per device.

v0:
```python
import jax
import jax.numpy as jnp
from jax import lax
from jax.sharding import PartitionSpec as P

logit_scale = 30.0


def normalize(proj):
    values = proj.astype(jnp.float32)
    norm = jnp.sqrt(jnp.sum(values * values, axis=1, keepdims=True) + 1e-06)
    return (values / norm, norm)


def orthonormal(matrix):
    count = matrix.shape[1]

    def column_step(k, basis):
        column = lax.dynamic_slice_in_dim(matrix, k, 1, 1)
        coeffs = jnp.dot(basis.T, column, precision=lax.Precision.HIGHEST)
        column = column - jnp.dot(basis, coeffs, precision=lax.Precision.HIGHEST)
        column = column / jnp.sqrt(jnp.sum(column * column) + 1e-06)
        return lax.dynamic_update_slice_in_dim(basis, column, k, 1)

    return lax.fori_loop(0, count, column_step, jnp.zeros(matrix.shape, jnp.float32))


def scores(left, right):
    return lax.dot_general(
        left, right, (((1,), (1,)), ((), ())), preferred_element_type=jnp.float32
    )


def inner(left, right):
    return lax.dot_general(
        left, right, (((0,), (0,)), ((), ())), preferred_element_type=jnp.float32
    )


def inner_exact(left, right):
    return lax.dot_general(
        left,
        right,
        (((0,), (0,)), ((), ())),
        precision=lax.Precision.HIGHEST,
        preferred_element_type=jnp.float32,
    )


def backnorm(unit, grad, norm):
    return ((grad - unit * jnp.sum(unit * grad, axis=1, keepdims=True)) / norm).astype(jnp.bfloat16)


def shards(
    audio_hidden, score_hidden, audio_proj, score_proj, labels, q_seed, err_audio, err_score
):
    tok_rows = audio_hidden.shape[0]
    first = lax.axis_index("con") * tok_rows
    unit_a, norm_a = normalize(audio_proj)
    unit_b, norm_b = normalize(score_proj)
    emb_a = unit_a.astype(jnp.bfloat16)
    emb_b = unit_b.astype(jnp.bfloat16)
    audio_all, score_all = (
        lax.all_gather(emb_a, "con", axis=0, tiled=True),
        lax.all_gather(emb_b, "con", axis=0, tiled=True),
    )
    partners = lax.all_gather(labels, "con", axis=1, tiled=True)[0]
    group_rows = audio_all.shape[0]
    rows_logits = logit_scale * scores(emb_a, score_all)
    cols_logits = logit_scale * scores(emb_b, audio_all)
    row_total = jnp.log(jnp.sum(jnp.exp(rows_logits), axis=1))
    col_total = jnp.log(jnp.sum(jnp.exp(cols_logits), axis=1))
    row_every, col_every = (
        lax.all_gather(row_total, "con", axis=0, tiled=True),
        lax.all_gather(col_total, "con", axis=0, tiled=True),
    )
    columns = jnp.arange(group_rows, dtype=jnp.int32)
    own_rows = first + jnp.arange(tok_rows, dtype=jnp.int32)
    hit_a = (labels[0][:, None] == columns[None, :]).astype(jnp.float32)
    hit_b = (partners[None, :] == own_rows[:, None]).astype(jnp.float32)
    weight_a = (
        0.5
        * (jnp.exp(rows_logits - row_total[:, None]) + jnp.exp(rows_logits - col_every[None, :]))
        - hit_a
    )
    weight_b = (
        0.5
        * (jnp.exp(cols_logits - col_total[:, None]) + jnp.exp(cols_logits - row_every[None, :]))
        - hit_b
    )
    grad_ea = logit_scale * jnp.dot(
        weight_a.astype(jnp.bfloat16), score_all, preferred_element_type=jnp.float32
    )
    grad_eb = logit_scale * jnp.dot(
        weight_b.astype(jnp.bfloat16), audio_all, preferred_element_type=jnp.float32
    )
    dz_a = backnorm(unit_a, grad_ea, norm_a)
    dz_b = backnorm(unit_b, grad_eb, norm_b)
    slab = err_audio.shape[1]
    grad_a = lax.psum_scatter(inner(audio_hidden, dz_a), "con", scatter_dimension=0, tiled=True)
    grad_b = lax.psum_scatter(inner(score_hidden, dz_b), "con", scatter_dimension=0, tiled=True)
    memory_a = grad_a + err_audio[0]
    memory_b = grad_b + err_score[0]
    part_a = jnp.dot(memory_a, q_seed, precision=lax.Precision.HIGHEST)
    part_b = jnp.dot(memory_b, q_seed, precision=lax.Precision.HIGHEST)
    left_a, left_b = lax.psum((part_a, part_b), "rep")
    full_a, full_b = (
        lax.all_gather(left_a, "con", axis=0, tiled=True),
        lax.all_gather(left_b, "con", axis=0, tiled=True),
    )
    row_start = lax.axis_index("con") * slab
    hat_a = lax.dynamic_slice_in_dim(orthonormal(full_a), row_start, slab, 0)
    hat_b = lax.dynamic_slice_in_dim(orthonormal(full_b), row_start, slab, 0)
    right_a, right_b = lax.psum(
        (inner_exact(memory_a, hat_a), inner_exact(memory_b, hat_b)), ("rep", "con")
    )
    replicas = lax.axis_size("rep")
    right_a = right_a / replicas
    right_b = right_b / replicas
    new_a = memory_a - jnp.dot(hat_a, right_a.T, precision=lax.Precision.HIGHEST)
    new_b = memory_b - jnp.dot(hat_b, right_b.T, precision=lax.Precision.HIGHEST)
    return (hat_a, right_a, new_a[None], hat_b, right_b, new_b[None])


def solution(mesh):
    placed = (
        P(("rep", "con"), None),
        P(("rep", "con"), None),
        P(("rep", "con"), None),
        P(("rep", "con"), None),
        P("rep", "con"),
        P(),
        P("rep", "con", None),
        P("rep", "con", None),
    )
    return jax.shard_map(
        shards,
        mesh=mesh,
        in_specs=placed,
        out_specs=(
            P("con", None),
            P(),
            P("rep", "con", None),
            P("con", None),
            P(),
            P("rep", "con", None),
        ),
        check_vma=False,
    )
```

profile of v0, /device:TPU:1, one launch (start us, length us, event | category | flops | bytes accessed | tf_op | source)
XLA Modules:
  0.0 936.3 jit_solution(10779092235034584204)
XLA Ops:
  7.3 1.2 fusion.17
  8.5 1.8 fusion.29
  10.4 1.1 fusion.18
  14.0 50.8 %all-reduce.2 = s32[2560]{0:T(1024)S(1)} all-reduce(s32[2560]{0:T(1024)S(1)} %dynamic-update-slice.2), channel_id=1, replica_groups=mesh['rep'=16,'con'=16] {'con'}, use_global_device_ids=true, to_apply=%add.2 | all-reduce | flops 2560 | bytes 20480
  64.9 5.7 exponential_reduce_fusion
  70.7 32.0 %all-gather.5.cloned.1.call-done = bf16[2560,1024]{1,0:T(8,128)(2,1)} async-done(((bf16[160,1024]{1,0:T(8,128)(2,1)}), bf16[2560,1024]{1,0:T(8,128)(2,1)}) %all-gather.5.cloned.1.call-update) | async-done | bytes 5242896 | tf_op jit(solution)/shard_map/all_gather | solution.py:65
  102.7 4.5 exponential_reduce_fusion.1
  107.4 44.4 %all-reduce.4 = (f32[2560]{0:T(1024)S(1)}, f32[2560]{0:T(1024)S(1)}) all-reduce(f32[2560]{0:T(1024)S(1)} %get-tuple-element.171, f32[2560]{0:T(1024)S(1)} %get-tuple-element.173), channel_id=1, replica_groups=mesh['rep'=16,'con'=16] {'con'}, use_global_device_ids=true, to_apply=%add | all-reduce | flops 5120 | bytes 40960
  151.7 4.5 multiply_reduce_fusion.2
  156.2 3.4 convolution_bitcast_fusion.4
  159.6 6.0 copy.36
  166.5 4.0 multiply_reduce_fusion.3
  170.6 3.4 convolution_bitcast_fusion.5
  173.9 5.9 copy.34
  179.9 49.0 %reduce-scatter.9.cloned.1.call-done = f32[80,1024]{1,0:T(8,128)} async-done(((f32[1280,1024]{1,0:T(8,128)}), f32[80,1024]{1,0:T(8,128)}) %reduce-scatter.9.cloned.1.call-update) | async-done | bytes 327696 | tf_op jit(solution)/shard_map/reduce_scatter | solution.py:101
  228.9 1.4 fusion.28
  230.3 64.4 %reduce-scatter.7.cloned.1.call-done = f32[80,1024]{1,0:T(8,128)} async-done(((f32[1280,1024]{1,0:T(8,128)}), f32[80,1024]{1,0:T(8,128)}) %reduce-scatter.7.cloned.1.call-update) | async-done | bytes 327696 | tf_op jit(solution)/shard_map/reduce_scatter | solution.py:100
  294.7 1.4 fusion.26
  296.1 60.7 %all-reduce.5 = (f32[80,64]{0,1:T(8,128)S(1)}, f32[80,64]{0,1:T(8,128)S(1)}) all-reduce(f32[80,64]{0,1:T(8,128)S(1)} %fusion.26, f32[80,64]{0,1:T(8,128)S(1)} %fusion.28), channel_id=1, replica_groups=mesh['rep'=16,'con'=16] {'rep'}, use_global_device_ids=true, to_apply=%region_6.0 | all-reduce | flops 10240 | bytes 81920 | tf_op jit(solution)/shard_map/psum | solution.py:106
  356.8 33.1 %all-gather.1 = f32[16,80,64]{1,2,0:T(8,128)S(1)} all-gather(f32[1,80,64]{1,2,0:T(8,128)S(1)} %bitcast.83), channel_id=1, replica_groups=mesh['rep'=16,'con'=16] {'con'}, dimensions={0}, use_global_device_ids=true | all-gather | bytes 348160 | tf_op jit(solution)/shard_map/all_gather | solution.py:109
  390.6 134.9 %while.27 = (s32[]{:T(128)}, f32[1280,64]{0,1:T(8,128)S(1)}, f32[1280,64]{0,1:T(8,128)S(1)}, s32[]{:T(128)}, f32[]{:T(128)}, /*index=5*/s32[]{:T(128)}) while((s32[]{:T(128)}, f32[1280,64]{0,1:T(8,128)S(1)}, f32[1280,64]{0,1:T(8,128)S(1)}, s32[]{:T(128)}, f32[]{:T(128)}, /*index=5*/s32[]{:T(128)}) %tuple.70), condition=%wide.region_16.0_spmd, body=%wide.region_14.16_spmd.sunk | while | flops 1971202 | bytes 691829 | solution.py:25
  403.6 0.9 multiply_reduce_fusion.7
  405.7 0.9 multiply_reduce_fusion.7
  525.5 17.4 %all-gather = f32[16,80,64]{1,2,0:T(8,128)S(1)} all-gather(f32[1,80,64]{1,2,0:T(8,128)S(1)} %bitcast.82), channel_id=1, replica_groups=mesh['rep'=16,'con'=16] {'con'}, dimensions={0}, use_global_device_ids=true | all-gather | bytes 348160 | tf_op jit(solution)/shard_map/all_gather | solution.py:108
  543.5 134.9 %while.26 = (s32[]{:T(128)}, f32[1280,64]{0,1:T(8,128)S(1)}, f32[1280,64]{0,1:T(8,128)S(1)}, s32[]{:T(128)}, f32[]{:T(128)}, /*index=5*/s32[]{:T(128)}) while((s32[]{:T(128)}, f32[1280,64]{0,1:T(8,128)S(1)}, f32[1280,64]{0,1:T(8,128)S(1)}, s32[]{:T(128)}, f32[]{:T(128)}, /*index=5*/s32[]{:T(128)}) %tuple.73), condition=%wide.region_9.0_spmd, body=%wide.region_7.9_spmd.sunk | while | flops 1971202 | bytes 691829 | solution.py:25
  678.6 1.1 fusion.27
  679.7 1.1 fusion.25
  680.8 244.5 %all-reduce.8.cloned.1.call-done = (f32[1024,64]{0,1:T(8,128)}, f32[1024,64]{0,1:T(8,128)}) async-done(((f32[1024,64]{0,1:T(8,128)}, f32[1024,64]{0,1:T(8,128)}), (f32[1024,64]{0,1:T(8,128)}, f32[1024,64]{0,1:T(8,128)})) %all-reduce.8.cloned.1.call-update) | async-done | bytes 524304 | tf_op jit(solution)/shard_map/psum | solution.py:114
  925.3 1.0 broadcast_multiply_fusion.1
  926.2 1.1 broadcast_multiply_fusion
  927.3 1.2 fusion.7
  928.5 1.2 fusion.6
  (571 shorter events, 179.8 us)
Async XLA Ops:
  7.2 149.0 %copy-start = (bf16[160,1280]{1,0:T(8,128)(2,1)S(1)}, bf16[160,1280]{1,0:T(8,128)(2,1)}, u32[]{:S(2)}) copy-start(bf16[160,1280]{1,0:T(8,128)(2,1)} %param.13) | copy-start | bytes 1228804
  7.2 5.3 copy-start.15
  7.2 4.3 copy-start.6
  7.2 6.5 copy-start.13
  7.2 57.6 %all-gather.7.cloned.1.call-start = ((), (), s32[]{:S(2)}) async-start(), calls=%async_computation.3 | async-start | bytes 5570560 | tf_op jit(solution)/shard_map/all_gather | solution.py:64
  10.3 92.4 %all-gather.5.cloned.1.call-start = ((), (), s32[]{:S(2)}) async-start(), calls=%async_computation.2 | async-start | bytes 5570560 | tf_op jit(solution)/shard_map/all_gather | solution.py:65
  12.4 216.5 %reduce-scatter.9.cloned.1.call-start = ((), (), s32[]{:S(2)}) async-start(), calls=%async_computation.5 | async-start | bytes 5570560 | tf_op jit(solution)/shard_map/reduce_scatter | solution.py:101
  64.9 37.9 %copy-start.5 = (bf16[160,1024]{1,0:T(8,128)(2,1)S(1)}, bf16[160,1024]{1,0:T(8,128)(2,1)}, u32[]{:S(2)}) copy-start(bf16[160,1024]{1,0:T(8,128)(2,1)} %fusion.29) | copy-start | bytes 983044
  165.5 1.0 copy-start.7
  165.6 129.1 %reduce-scatter.7.cloned.1.call-start = ((), (), s32[]{:S(2)}) async-start(), calls=%async_computation.4 | async-start | bytes 5570560 | tf_op jit(solution)/shard_map/reduce_scatter | solution.py:100
  166.5 4.1 copy-start.14
  179.9 49.0 %copy-start.2 = (f32[1,80,1024]{2,1,0:T(8,128)S(1)}, f32[1,80,1024]{2,1,0:T(8,128)}, u32[]{:S(2)}) copy-start(f32[1,80,1024]{2,1,0:T(8,128)} %param.19) | copy-start | bytes 983044
  179.9 49.0 %copy-start.10 = (f32[1024,64]{0,1:T(8,128)S(1)}, f32[1024,64]{0,1:T(8,128)}, u32[]{:S(2)}) copy-start(f32[1024,64]{0,1:T(8,128)} %param.17) | copy-start | bytes 786436
  179.9 114.8 %copy-start.1 = (f32[1,80,1024]{2,1,0:T(8,128)S(1)}, f32[1,80,1024]{2,1,0:T(8,128)}, u32[]{:S(2)}) copy-start(f32[1,80,1024]{2,1,0:T(8,128)} %param.18) | copy-start | bytes 983044
  179.9 745.4 %all-reduce.8.cloned.1.call-start = ((), (), s32[]{:S(2)}) async-start(), calls=%async_computation.6 | async-start | bytes 1048576 | tf_op jit(solution)/shard_map/psum | solution.py:114
  543.5 135.1 %copy-start.3 = (f32[80,1024]{1,0:T(8,128)S(1)}, f32[80,1024]{1,0:T(8,128)}, u32[]{:S(2)}) copy-start(f32[80,1024]{1,0:T(8,128)} %reduce-scatter.9.cloned.1.call-done) | copy-start | bytes 983044
  543.5 136.2 %copy-start.4 = (f32[80,1024]{1,0:T(8,128)S(1)}, f32[80,1024]{1,0:T(8,128)}, u32[]{:S(2)}) copy-start(f32[80,1024]{1,0:T(8,128)} %reduce-scatter.7.cloned.1.call-done) | copy-start | bytes 983044
  678.5 248.8 %copy-start.12 = (f32[80,64]{0,1:T(8,128)}, f32[80,64]{0,1:T(8,128)S(1)}, u32[]{:S(2)}) copy-start(f32[80,64]{0,1:T(8,128)S(1)} %get-tuple-element.183) | copy-start | bytes 61444
  678.6 250.0 %copy-start.11 = (f32[80,64]{0,1:T(8,128)}, f32[80,64]{0,1:T(8,128)S(1)}, u32[]{:S(2)}) copy-start(f32[80,64]{0,1:T(8,128)S(1)} %get-tuple-element.182) | copy-start | bytes 61444
  926.2 3.5 copy-start.8
  927.3 2.4 copy-start.9
Sparse Core Ops, SparseCore 0:
  10.5 47.9 all-gather.6
  60.9 41.7 all-gather.4
  165.7 63.1 reduce-scatter.8
  231.3 63.3 reduce-scatter.6
  680.9 244.2 all-reduce.7
where the time goes:
time: 939 us; the launch traced here: 936 us
  waiting for transfers between devices  390 us (42%)
  blocking collectives  206 us (22%)
  matrix products  192 us (20%)
  loops' own time  92.8 us (10%)
  local copies, waits for them, and re-layouts  32.4 us (3%)
  between operations  14.7 us (2%)
    psum x1, waiting for transfers between devices, shards(): lax.psum((inner_exact(memory_a, hat_a), inner_exact(memory_b, hat_b)), ('...  244 us
    dot_general x128, matrix products, column_step(): column = column - jnp.dot(basis, coeffs, precision=lax.Precision.HIGHEST)  116 us
    unnamed x2, blocking collectives  95.2 us
    another operation x2, loops' own time, orthonormal(): lax.fori_loop(0, count, column_step, jnp.zeros(matrix.shape, jnp.float32))  92.8 us
    reduce_scatter x1, waiting for transfers between devices, shards(): lax.psum_scatter(inner(audio_hidden, dz_a), 'con', scatter_dimension=0, t...  64.4 us
    psum x1, blocking collectives, shards(): left_a, left_b = lax.psum((part_a, part_b), 'rep')  60.7 us
    reduce_scatter x1, waiting for transfers between devices, shards(): lax.psum_scatter(inner(score_hidden, dz_b), 'con', scatter_dimension=0, t...  49 us
    dot_general x128, matrix products, column_step(): coeffs = jnp.dot(basis.T, column, precision=lax.Precision.HIGHEST)  42.4 us
  transfers between devices with their start and end apart: 5, of which 4 were waited for; matrix products, arithmetic and copies ran while one was open for 2% of the time, Pallas kernels for 0%

commit v1 on v0

v1 whole, which is shorter than its diff:
```python
import functools

import jax
import jax.numpy as jnp
from jax import lax
from jax.experimental import pallas as pl
from jax.experimental.pallas import tpu as pltpu
from jax.sharding import PartitionSpec as P

MESH = pl.DeviceIdType.MESH
logit_scale = 30.0
NORM_EPS = 1e-06
NT = (((1,), (1,)), ((), ()))
TN = (((0,), (0,)), ((), ()))
NN = (((1,), (0,)), ((), ()))
HIGH = lax.Precision.HIGHEST

SLOT_OF = (0, 1, 3, 5, 7, 6, 4, 2)
BEHIND = (0, 1, 7, 2, 6, 3, 5, 4)
RING = (
    ((1, 0), (1, 1), (2, 0), (2, 1), (3, 0), (3, 1), (4, 0)),
    ((1, 1), (1, 0), (2, 1), (2, 0), (3, 1), (3, 0), (4, 1)),
)


def exact(left, right, dims):
    return lax.dot_general(
        left, right, dims, precision=HIGH, preferred_element_type=jnp.float32
    )


def grads_kernel(
    n_z, proj_a, proj_b, labels, hidden_a, hidden_b, err_a, err_b,
    mem_ref,
    raw, emb, logit, weight, grad, row_sum, col_sum, row_info, col_id, lab, stage, hid, err,
    ring_send, ring_recv, sib_send, sib_recv, lab_send, lab_recv, hid_send, hid_recv,
    err_send, err_recv, local_sem,
):
    tok = proj_a.shape[0]
    chip = 2 * tok
    width = proj_a.shape[1]
    group = raw.shape[1]
    feat = hid.shape[1]
    slab = err_a.shape[1]
    rep = lax.axis_index("rep")
    con = lax.axis_index("con")
    z = con // 2
    core = lax.rem(con, 2)
    other = 1 - core

    def device(ahead, cross):
        where = lax.rem(z + ahead, n_z)
        return (rep, where * 2 + (other if cross else core))

    partners = [(o, r) for o in range(n_z) for r in range(2) if (o, r) != (0, 0)]

    projs = (proj_a, proj_b)
    loads = [
        pltpu.make_async_copy(projs[t], raw.at[t, pl.ds(0, tok), :], local_sem.at[t])
        for t in range(2)
    ]
    for load in loads:
        load.start()
    errs = (err_a, err_b)

    barrier = pltpu.get_barrier_semaphore()
    for o, r in partners:
        pl.semaphore_signal(barrier, inc=1, device_id=device(o, r), device_id_type=MESH)
    pl.semaphore_wait(barrier, len(partners))
    for load in loads:
        load.wait()

    def ring(way, n):
        dist, t = RING[way][n]
        source = SLOT_OF[dist - 1] if way == 0 else SLOT_OF[(n_z - dist + 1) % n_z]
        target = SLOT_OF[dist] if way == 0 else SLOT_OF[n_z - dist]
        return pltpu.make_async_remote_copy(
            src_ref=raw.at[t, pl.ds(source * chip, tok), :],
            dst_ref=raw.at[t, pl.ds(target * chip, tok), :],
            send_sem=ring_send.at[way, n],
            recv_sem=ring_recv.at[way, n],
            device_id=device(1 if way == 0 else n_z - 1, 0),
            device_id_type=MESH,
        )

    def sib(way, n):
        if n < 0:
            slot, t, index = 0, way, 7
        else:
            dist, t = RING[way][n]
            slot, index = (SLOT_OF[dist] if way == 0 else SLOT_OF[n_z - dist]), n
        return pltpu.make_async_remote_copy(
            src_ref=raw.at[t, pl.ds(slot * chip, tok), :],
            dst_ref=raw.at[t, pl.ds(slot * chip + tok, tok), :],
            send_sem=sib_send.at[way, index],
            recv_sem=sib_recv.at[way, index],
            device_id=device(0, 1),
            device_id_type=MESH,
        )

    def label_copy(o, r):
        return pltpu.make_async_remote_copy(
            src_ref=labels,
            dst_ref=lab.at[SLOT_OF[o], r],
            send_sem=lab_send.at[o, r],
            recv_sem=lab_recv.at[o, r],
            device_id=device(o, r),
            device_id_type=MESH,
        )

    def hidden_copy(o, r):
        return pltpu.make_async_remote_copy(
            src_ref=stage.at[other if r else core, lax.rem(z + o, n_z)],
            dst_ref=hid.at[pl.ds(SLOT_OF[o] * chip + r * tok, tok), :],
            send_sem=hid_send.at[o, r],
            recv_sem=hid_recv.at[o, r],
            device_id=device(o, r),
            device_id_type=MESH,
        )

    def err_copy(t):
        return pltpu.make_async_remote_copy(
            src_ref=errs[t].at[0],
            dst_ref=err.at[1],
            send_sem=err_send,
            recv_sem=err_recv,
            device_id=device(0, 1),
            device_id_type=MESH,
        )

    def err_local(t):
        return pltpu.make_async_copy(errs[t].at[0], err.at[0], local_sem.at[2])

    def normalize(slot, cross, t):
        rows = pl.ds(slot * chip + cross * tok, tok)
        values = raw[t, rows, :].astype(jnp.float32)
        inverse = lax.rsqrt(jnp.sum(values * values, axis=1, keepdims=True) + NORM_EPS)
        emb[t, rows, :] = (values * inverse).astype(jnp.bfloat16)
        row_info[rows, t : t + 1] = inverse

    for way in range(2):
        ring(way, 0).start()
    for way in range(2):
        ring(way, 1).start()
    for t in range(2):
        sib(t, -1).start()
    for o, r in partners:
        label_copy(o, r).start()

    @pl.when(core == 0)
    def _():
        err_copy(1).start()
        err_local(0).start()

    @pl.when(core == 1)
    def _():
        err_copy(0).start()
        err_local(1).start()

    lab[0, 0] = labels[...]
    row_sum[...] = jnp.zeros_like(row_sum)
    col_sum[...] = jnp.zeros_like(col_sum)
    for t in range(2):
        normalize(0, 0, t)
    for t, hidden in enumerate((hidden_a, hidden_b)):
        for k in range(n_z):
            stage[t, k] = hidden[:, k * feat : (k + 1) * feat]

    tile = 256

    def tile_logits(r0, c0):
        x = emb[core, pl.ds(r0, tile), :]
        y = emb[other, pl.ds(c0, tile), :]
        part = jnp.exp(
            logit_scale * lax.dot_general(x, y, NT, preferred_element_type=jnp.float32)
        )
        logit[pl.ds(r0, tile), pl.ds(c0, tile)] = part
        lanes = part[:, 0:128]
        for k in range(1, tile // 128):
            lanes = lanes + part[:, k * 128 : (k + 1) * 128]
        row_sum[pl.ds(r0, tile), :] += lanes
        col_sum[:, pl.ds(c0, tile)] += jnp.sum(part.reshape(tile // 8, 8, tile), axis=0)

    def logits_to(old, new):
        def columns(k, _):
            c0 = pl.multiple_of(old + (k // (new // tile)) * tile, tile)
            r0 = pl.multiple_of(lax.rem(k, new // tile) * tile, tile)
            tile_logits(r0, c0)
            return 0

        lax.fori_loop(0, ((new - old) // tile) * (new // tile), columns, 0)
        if old:

            def rows(k, _):
                c0 = pl.multiple_of((k // ((new - old) // tile)) * tile, tile)
                r0 = pl.multiple_of(old + lax.rem(k, (new - old) // tile) * tile, tile)
                tile_logits(r0, c0)
                return 0

            lax.fori_loop(0, ((new - old) // tile) * (old // tile), rows, 0)

    last = len(RING[0])
    bounds = [chip * k // tile * tile for k in (3, 5, 7)]
    done = 0
    for n in range(last):
        for way in range(2):
            ring(way, n).wait_recv()
            if n + 2 < last:
                ring(way, n + 2).start()
            sib(way, n).start()
        for way in range(2):
            dist, t = RING[way][n]
            normalize(SLOT_OF[dist] if way == 0 else SLOT_OF[n_z - dist], 0, t)
            sib(way, n - 1).wait_recv()
            if n == 0:
                normalize(0, 1, way)
            else:
                dist, t = RING[way][n - 1]
                normalize(SLOT_OF[dist] if way == 0 else SLOT_OF[n_z - dist], 1, t)
        if n == last - 1:
            for o, r in partners:
                hidden_copy(o, r).start()
        if n in (2, 4, 6):
            logits_to(done, bounds[n // 2 - 1])
            done = bounds[n // 2 - 1]
    for way in range(2):
        sib(way, last - 1).wait_recv()
        dist, t = RING[way][last - 1]
        normalize(SLOT_OF[dist] if way == 0 else SLOT_OF[n_z - dist], 1, t)

    for o, r in partners:
        label_copy(o, r).wait_recv()
    for slot in range(n_z):
        where = lax.rem(z + n_z - BEHIND[slot], n_z)
        for r in range(2):
            first = ((where * 2 + (other if r else core)) * tok).astype(jnp.float32)
            piece = lab[slot, r]
            spread = jnp.broadcast_to(piece[0:1, :], (128, piece.shape[1])).T[:tok, 0:1]
            own = first + lax.broadcasted_iota(jnp.int32, (tok, 1), 0).astype(jnp.float32)
            rows = pl.ds(slot * chip + r * tok, tok)
            row_info[rows, 2:3] = jnp.where(core == 0, spread, own)
            row_info[rows, 3:4] = jnp.where(core == 0, own, spread)
    for k in range(group // 128):
        ids = row_info[k * 128 : (k + 1) * 128, 3:4]
        col_id[:, k * 128 : (k + 1) * 128] = jnp.broadcast_to(ids, (128, 128)).T[0:8, :]

    logits_to(done, group)

    row_info[:, 4:5] = 0.5 / jnp.sum(row_sum[...], axis=1, keepdims=True)
    col_sum[0:1, :] = 0.5 / jnp.sum(col_sum[...], axis=0, keepdims=True)
    row_info[:, 5:6] = jnp.where(core == 0, row_info[:, 0:1], row_info[:, 1:2])

    chunk = weight.shape[0]
    fine = 16

    def chunk_step(k, _):
        r0 = pl.multiple_of(k * chunk, chunk)

        def weights(m, _):
            rows = pl.ds(pl.multiple_of(r0 + m * fine, fine), fine)
            base = row_info[rows, 4:5]
            ids = row_info[rows, 2:3]
            value = logit[rows, :] * (base + col_sum[0:1, :])
            value = value - jnp.where(ids == col_id[0:1, :], 1.0, 0.0)
            weight[pl.ds(pl.multiple_of(m * fine, fine), fine), :] = value.astype(jnp.bfloat16)
            return 0

        lax.fori_loop(0, chunk // fine, weights, 0)
        grad[...] = lax.dot_general(
            weight[...], emb[other], NN, preferred_element_type=jnp.float32
        )

        def finish(m, _):
            rows = pl.ds(pl.multiple_of(r0 + m * fine, fine), fine)
            inverse = row_info[rows, 5:6]
            unit = raw[core, rows, :].astype(jnp.float32) * inverse
            value = logit_scale * grad[pl.ds(pl.multiple_of(m * fine, fine), fine), :]
            along = jnp.sum(unit * value, axis=1, keepdims=True)
            emb[core, rows, :] = ((value - unit * along) * inverse).astype(jnp.bfloat16)
            return 0

        lax.fori_loop(0, chunk // fine, finish, 0)
        return 0

    lax.fori_loop(0, group // chunk, chunk_step, 0)

    hid[0:tok, :] = stage[core, z]
    for o, r in partners:
        hidden_copy(o, r).wait_recv()
    err_copy(0).wait_recv()
    err_local(0).wait()
    total = lax.dot_general(hid[...], emb[core], TN, preferred_element_type=jnp.float32)
    for k in range(2):
        rows = slice(k * slab, (k + 1) * slab)
        mem_ref[rows, :] = total[rows, :] + err[jnp.where(core == k, 0, 1)]

    for way in range(2):
        for n in range(last):
            ring(way, n).wait_send()
            sib(way, n).wait_send()
        sib(way, -1).wait_send()
    for o, r in partners:
        label_copy(o, r).wait_send()
        hidden_copy(o, r).wait_send()
    err_copy(0).wait_send()


def head_gradient(n_z, proj_a, proj_b, labels, hidden_a, hidden_b, err_a, err_b):
    tok, width = proj_a.shape
    group = tok * n_z * 2
    feat = hidden_a.shape[1] // n_z
    slab = err_a.shape[1]
    wide = labels.shape[1]
    chunk = 256
    dma = pltpu.SemaphoreType.DMA
    any_space = pl.BlockSpec(memory_space=pl.ANY)
    vmem = pl.BlockSpec(memory_space=pltpu.VMEM)
    return pl.pallas_call(
        functools.partial(grads_kernel, n_z),
        out_shape=jax.ShapeDtypeStruct((feat, width), jnp.float32),
        in_specs=[any_space, any_space, vmem, vmem, vmem, any_space, any_space],
        out_specs=vmem,
        scratch_shapes=[
            pltpu.VMEM((2, group, width), jnp.bfloat16),
            pltpu.VMEM((2, group, width), jnp.bfloat16),
            pltpu.VMEM((group, group), jnp.float32),
            pltpu.VMEM((chunk, group), jnp.bfloat16),
            pltpu.VMEM((chunk, width), jnp.float32),
            pltpu.VMEM((group, 128), jnp.float32),
            pltpu.VMEM((8, group), jnp.float32),
            pltpu.VMEM((group, 128), jnp.float32),
            pltpu.VMEM((8, group), jnp.float32),
            pltpu.VMEM((n_z, 2, 8, wide), jnp.float32),
            pltpu.VMEM((2, n_z, tok, feat), jnp.bfloat16),
            pltpu.VMEM((group, feat), jnp.bfloat16),
            pltpu.VMEM((2, slab, width), jnp.float32),
            dma((2, 7)),
            dma((2, 7)),
            dma((2, 8)),
            dma((2, 8)),
            dma((n_z, 2)),
            dma((n_z, 2)),
            dma((n_z, 2)),
            dma((n_z, 2)),
            dma,
            dma,
            dma((3,)),
        ],
        compiler_params=pltpu.CompilerParams(
            collective_id=0, has_side_effects=True, vmem_limit_bytes=63 * 1024 * 1024
        ),
        name="head_gradient",
    )(proj_a, proj_b, labels, hidden_a, hidden_b, err_a, err_b)


def compress_kernel(
    n_y, n_x, n_z, mem, seed,
    p_ref, q_ref, new_ref,
    mem_sib, x_buf, y_buf, g_buf, part, gathered, z_buf, full, state, basis, q_own, q_sib, p_own, p_sib,
    x_send, x_recv, y_send, y_recv, g_send, g_recv, r_send, r_recv, z_send, z_recv,
    f_send, f_recv, sib_send, sib_recv,
):
    n_rep = n_y * n_x
    slab = mem_sib.shape[0]
    rank = seed.shape[1]
    width = mem.shape[1]
    rep = lax.axis_index("rep")
    con = lax.axis_index("con")
    y = rep // n_x
    x = lax.rem(rep, n_x)
    z = con // 2
    core = lax.rem(con, 2)
    other = 1 - core
    sibling = (rep, z * 2 + other)

    def along_x(i):
        return (y * n_x + lax.rem(x + i, n_x), con)

    def along_y(i):
        return (lax.rem(y + i, n_y) * n_x + x, con)

    def along_z(i):
        return (rep, lax.rem(z + i, n_z) * 2 + core)

    def along_rep(i):
        return (lax.rem(rep + i, n_rep), con)

    barrier = pltpu.get_barrier_semaphore()
    greet = [along_rep(i) for i in range(1, n_rep)] + [along_z(i) for i in range(1, n_z)]
    for peer in greet + [sibling]:
        pl.semaphore_signal(barrier, inc=1, device_id=peer, device_id_type=MESH)
    pl.semaphore_wait(barrier, len(greet) + 1)

    def copy(source, target, send, recv, peer):
        return pltpu.make_async_remote_copy(
            src_ref=source, dst_ref=target, send_sem=send, recv_sem=recv,
            device_id=peer, device_id_type=MESH,
        )

    theirs = pl.ds(pl.multiple_of(other * slab, 8), slab)
    ours = pl.ds(pl.multiple_of(core * slab, 8), slab)
    mem_copy = copy(mem.at[theirs, :], mem_sib, sib_send.at[0], sib_recv.at[0], sibling)
    mem_copy.start()

    def all_sum(buf, index, count, send, recv, peers, value):
        buf[index] = value
        copies = [
            copy(buf.at[index], buf.at[index], send.at[i], recv.at[i], peers(i))
            for i in range(1, count)
        ]
        for one in copies:
            one.start()

        def finish():
            for one in copies:
                one.wait()
            total = buf[0]
            for k in range(1, count):
                total = total + buf[k]
            return total

        return finish

    left = exact(mem[...], seed[...], NN)
    packed = jnp.concatenate([left[:slab, :], left[slab:, :]], axis=1)
    packed = all_sum(x_buf, x, n_x, x_send, x_recv, along_x, packed)()
    packed = all_sum(y_buf, y, n_y, y_send, y_recv, along_y, packed)()
    left = jnp.concatenate([packed[:, :rank], packed[:, rank:]], axis=0)

    gram = exact(left, left, TN)
    gram_sum = all_sum(
        g_buf, z, n_z, g_send, g_recv, along_z,
        jnp.concatenate([gram[: rank // 2, :], gram[rank // 2 :, :]], axis=1),
    )
    right = exact(left, mem[...], TN)
    span = width // 2
    for k in range(n_rep):
        part[k] = right[8 * (k // 2) : 8 * (k // 2) + 8, span * (k % 2) : span * (k % 2) + span]
    gathered[rep] = part[rep]
    reduce = [
        copy(
            part.at[lax.rem(rep + i, n_rep)], gathered.at[rep], r_send.at[i], r_recv.at[i],
            along_rep(i),
        )
        for i in range(1, n_rep)
    ]
    for one in reduce:
        one.start()

    gram = gram_sum()
    gram = jnp.concatenate([gram[:, :rank], gram[:, rank:]], axis=0)
    eye = (
        lax.broadcasted_iota(jnp.int32, (rank, rank), 0)
        == lax.broadcasted_iota(jnp.int32, (rank, rank), 1)
    ).astype(jnp.float32)
    state[...] = jnp.concatenate([eye, gram], axis=1)

    def column_step(k, _):
        value = state[...]
        row = state[pl.ds(k, 1), :]
        lane_row = lax.broadcasted_iota(jnp.int32, (1, 2 * rank), 1)
        lane = lax.broadcasted_iota(jnp.int32, (rank, 2 * rank), 1)
        product = jnp.where(lane_row < rank, row * pltpu.roll(row, rank, 1), 0.0)
        square = jnp.maximum(jnp.sum(product, axis=1, keepdims=True), 0.0) + NORM_EPS
        column = jnp.sum(jnp.where(lane == rank + k, value, 0.0), axis=1, keepdims=True)
        basis[pl.ds(k, 1), :] = row * lax.rsqrt(square)
        state[...] = value - column * (row / square)
        return 0

    cuts = [0, rank // 3, 2 * rank // 3, rank]
    lax.fori_loop(cuts[0], cuts[1], column_step, 0)
    for one in reduce:
        one.wait()
    total = gathered[0]
    for k in range(1, n_rep):
        total = total + gathered[k]
    z_sum = all_sum(z_buf, z, n_z, z_send, z_recv, along_z, total)
    lax.fori_loop(cuts[1], cuts[2], column_step, 0)
    full[rep] = z_sum()
    spread = [
        copy(full.at[rep], full.at[rep], f_send.at[i], f_recv.at[i], along_rep(i))
        for i in range(1, n_rep)
    ]
    for one in spread:
        one.start()
    lax.fori_loop(cuts[2], cuts[3], column_step, 0)

    turn = basis[:, :rank]
    p_own[...] = exact(left, turn, NT)
    p_copy = copy(p_own.at[theirs, :], p_sib, sib_send.at[1], sib_recv.at[1], sibling)
    p_copy.start()
    for one in spread:
        one.wait()
    right = jnp.concatenate(
        [jnp.concatenate([full[2 * k], full[2 * k + 1]], axis=1) for k in range(n_rep // 2)],
        axis=0,
    )
    q_own[...] = exact(turn, right, NN) / n_rep
    q_copy = copy(q_own, q_sib, sib_send.at[2], sib_recv.at[2], sibling)
    q_copy.start()
    new_ref[core] = mem[ours, :] - exact(p_own[ours, :], q_own[...], NN)
    p_ref[core] = p_own[ours, :]
    q_ref[core] = q_own[...].T
    mem_copy.wait()
    p_copy.wait()
    q_copy.wait()
    new_ref[other] = mem_sib[...] - exact(p_sib[...], q_sib[...], NN)
    p_ref[other] = p_sib[...]
    q_ref[other] = q_sib[...].T


def compress(n_y, n_x, n_z, mem, seed):
    feat, width = mem.shape
    rank = seed.shape[1]
    slab = feat // 2
    n_rep = n_y * n_x
    dma = pltpu.SemaphoreType.DMA
    vmem = pl.BlockSpec(memory_space=pltpu.VMEM)
    f32 = jnp.float32
    return pl.pallas_call(
        functools.partial(compress_kernel, n_y, n_x, n_z),
        out_shape=(
            jax.ShapeDtypeStruct((2, slab, rank), f32),
            jax.ShapeDtypeStruct((2, width, rank), f32),
            jax.ShapeDtypeStruct((2, slab, width), f32),
        ),
        in_specs=[vmem] * 2,
        out_specs=[vmem] * 3,
        scratch_shapes=[
            pltpu.VMEM((slab, width), f32),
            pltpu.VMEM((n_x, slab, 2 * rank), f32),
            pltpu.VMEM((n_y, slab, 2 * rank), f32),
            pltpu.VMEM((n_z, rank // 2, 2 * rank), f32),
            pltpu.VMEM((n_rep, 8, width // 2), f32),
            pltpu.VMEM((n_rep, 8, width // 2), f32),
            pltpu.VMEM((n_z, 8, width // 2), f32),
            pltpu.VMEM((n_rep, 8, width // 2), f32),
            pltpu.VMEM((rank, 2 * rank), f32),
            pltpu.VMEM((rank, 2 * rank), f32),
            pltpu.VMEM((rank, width), f32),
            pltpu.VMEM((rank, width), f32),
            pltpu.VMEM((feat, rank), f32),
            pltpu.VMEM((slab, rank), f32),
            dma((n_x,)), dma((n_x,)),
            dma((n_y,)), dma((n_y,)),
            dma((n_z,)), dma((n_z,)),
            dma((n_rep,)), dma((n_rep,)),
            dma((n_z,)), dma((n_z,)),
            dma((n_rep,)), dma((n_rep,)),
            dma((3,)), dma((3,)),
        ],
        compiler_params=pltpu.CompilerParams(
            collective_id=1, has_side_effects=True, vmem_limit_bytes=32 * 1024 * 1024
        ),
        name="compress",
    )(mem, seed)


def shards(
    audio_hidden, score_hidden, audio_proj, score_proj, labels, q_seed, err_audio, err_score
):
    n_z = 8
    n_y = n_x = 4
    tok = labels.shape[1]
    wide = -(-tok // 128) * 128
    spread = jnp.pad(labels.astype(jnp.float32), ((0, 7), (0, wide - tok)))
    mem = head_gradient(
        n_z, audio_proj, score_proj, spread, audio_hidden, score_hidden, err_audio, err_score
    )
    p, q, new = compress(n_y, n_x, n_z, mem, q_seed)
    return (p[0], q[0], new[0:1], p[1], q[1], new[1:2])


def solution(mesh):
    placed = (
        P(("rep", "con"), None),
        P(("rep", "con"), None),
        P(("rep", "con"), None),
        P(("rep", "con"), None),
        P("rep", "con"),
        P(),
        P("rep", "con", None),
        P("rep", "con", None),
    )
    return jax.shard_map(
        shards,
        mesh=mesh,
        in_specs=placed,
        out_specs=(
            P("con", None),
            P(),
            P("rep", "con", None),
            P("con", None),
            P(),
            P("rep", "con", None),
        ),
        check_vma=False,
    )
```

time: 939 us -> 199 us (0.21)
  waiting for transfers between devices: 390 us -> 0 us
  blocking collectives: 206 us -> 0 us
  matrix products: 192 us -> 0 us
  Pallas kernels: 0 us -> 190 us
  loops' own time: 92.8 us -> 0 us
  local copies, waits for them, and re-layouts: 32.4 us -> 6.95 us
  between operations: 14.7 us -> 0.68 us
    psum x1 -> x0, waiting for transfers between devices: 244 us -> none  [shards(): lax.psum((inner_exact(memory_a, hat_a), inner_exact(memory_b, hat_b)), ('...]
    dot_general x268 -> x0, matrix products: 192 us -> none  [the longest x128 116 us: column_step(): column = column - jnp.dot(basis, coeffs, precision=lax.Precision.HIGHEST)]
    pallas_call x0 -> x2, Pallas kernels: none -> 190 us  [the longest x1 152 us: head_gradient(): pl.pallas_call(functools.partial(grads_kernel, n_z), out_shape=jax.ShapeD...]
    reduce_scatter x2 -> x0, waiting for transfers between devices: 113 us -> none  [the longest x1 64.4 us: shards(): lax.psum_scatter(inner(audio_hidden, dz_a), 'con', scatter_dimension=0, t...]
    unnamed x2 -> x0, blocking collectives: 95.2 us -> none
    another operation x2 -> x0, loops' own time: 92.8 us -> none  [orthonormal(): lax.fori_loop(0, count, column_step, jnp.zeros(matrix.shape, jnp.float32))]
    psum x1 -> x0, blocking collectives: 60.7 us -> none  [shards(): left_a, left_b = lax.psum((part_a, part_b), 'rep')]
    all_gather x2 -> x0, blocking collectives: 50.6 us -> none  [the longest x1 33.1 us: shards(): lax.all_gather(left_b, 'con', axis=0, tiled=True)]
  transfers between devices with their start and end apart: 5 -> 0, of which waited for: 4 -> 0; matrix products, arithmetic and copies ran while one was open for 2% -> 0% of each run, Pallas kernels for 0% -> 0%
where the time goes in v1:
time: 199 us
  Pallas kernels  190 us (95%)
  local copies, waits for them, and re-layouts  6.95 us (3%)
    pallas_call x1, Pallas kernels, head_gradient(): pl.pallas_call(functools.partial(grads_kernel, n_z), out_shape=jax.ShapeD...  152 us
    pallas_call x1, Pallas kernels, compress(): pl.pallas_call(functools.partial(compress_kernel, n_y, n_x, n_z), out_sha...  38.9 us
    unnamed x7, local copies, waits for them, and re-layouts  5.39 us

profile of v1, /device:TPU:1, one launch (start us, length us, event | category | flops | bytes accessed | tf_op | source)
XLA Modules:
  0.0 198.7 jit_solution(13832889193343799361)
XLA Ops:
  0.6 0.7 convert_element_type.5
  1.3 0.6 pad.4.labels
  1.9 1.1 copy.14.seed
  3.1 151.5 %head_gradient.1.mem = f32[160,1024]{1,0:T(8,128)} custom-call(bf16[160,1024]{1,0:T(8,128)(2,1)} %proj_a.1, bf16[160,1024]{1,0:T(8,128)(2,1)} %proj_b.1, f32[8,256]{1,0:T(8,128)} %pad.4.labels, bf16[160,1280]{1,0:T(8,128)(2,1)} %hidden_a.1, bf16[160,1280]{1,0:T(8,128)(2,1)} %hidden_b.1, f32[1,80,1024]{2,1,0:T(8,128)} %err_a.1, f32[1,80,1024]{2,1,0:T(8,128)} %err_b.1), custom_call_target="tpu_custom_call" | custom-call | tf_op jit(solution)/shard_map/head_gradient/pallas_call | solution.py:318
  154.6 0.0 copy-start
  154.6 1.1 copy-done
  155.7 38.9 %compress.1 = (f32[2,80,64]{2,1,0:T(8,128)S(1)}, f32[2,1024,64]{2,1,0:T(8,128)S(1)}, f32[2,80,1024]{2,1,0:T(8,128)S(1)}) custom-call(f32[160,1024]{1,0:T(8,128)S(1)} %copy-done, f32[1024,64]{1,0:T(8,128)S(1)} %copy.14.seed), custom_call_target="tpu_custom_call" | custom-call | tf_op jit(solution)/shard_map/compress/pallas_call | solution.py:520
  194.6 0.7 copy.17
  195.3 0.7 copy.15
  196.0 0.9 fusion
  196.9 0.1 slice_bitcast_fusion
  196.9 0.9 copy.18
  197.8 0.9 copy.16
  (1 shorter events, 0.0 us)
Async XLA Ops:
  154.6 1.1 copy-start

commit v2 on v1

--- a/solution.py
+++ b/solution.py
@@ -10,6 +10,7 @@
 MESH = pl.DeviceIdType.MESH
 logit_scale = 30.0
 NORM_EPS = 1e-06
+LOG2E = 1.4426950408889634
 NT = (((1,), (1,)), ((), ()))
 TN = (((0,), (0,)), ((), ()))
 NN = (((1,), (0,)), ((), ()))
@@ -32,13 +33,13 @@
 def grads_kernel(
     n_z, proj_a, proj_b, labels, hidden_a, hidden_b, err_a, err_b,
     mem_ref,
-    raw, emb, logit, weight, grad, row_sum, col_sum, row_info, col_id, lab, stage, hid, err,
+    raw, emb, logit, weight, grad, row_sum, col_sum, row_info, col_id, lab, pair, stage, blocks,
+    hid, err,
     ring_send, ring_recv, sib_send, sib_recv, lab_send, lab_recv, hid_send, hid_recv,
-    err_send, err_recv, local_sem,
+    near_send, near_recv, local_sem,
 ):
     tok = proj_a.shape[0]
     chip = 2 * tok
-    width = proj_a.shape[1]
     group = raw.shape[1]
     feat = hid.shape[1]
     slab = err_a.shape[1]
@@ -48,11 +49,10 @@
     core = lax.rem(con, 2)
     other = 1 - core
 
-    def device(ahead, cross):
-        where = lax.rem(z + ahead, n_z)
-        return (rep, where * 2 + (other if cross else core))
-
-    partners = [(o, r) for o in range(n_z) for r in range(2) if (o, r) != (0, 0)]
+    def plane(ahead):
+        return (rep, lax.rem(z + ahead, n_z) * 2 + core)
+
+    sibling = (rep, z * 2 + other)
 
     projs = (proj_a, proj_b)
     loads = [
@@ -61,75 +61,69 @@
     ]
     for load in loads:
         load.start()
-    errs = (err_a, err_b)
 
     barrier = pltpu.get_barrier_semaphore()
-    for o, r in partners:
-        pl.semaphore_signal(barrier, inc=1, device_id=device(o, r), device_id_type=MESH)
-    pl.semaphore_wait(barrier, len(partners))
+    for peer in (plane(1), plane(n_z - 1), sibling):
+        pl.semaphore_signal(barrier, inc=1, device_id=peer, device_id_type=MESH)
+    pl.semaphore_wait(barrier, 3)
     for load in loads:
         load.wait()
 
+    def remote(source, target, send, recv, peer):
+        return pltpu.make_async_remote_copy(
+            src_ref=source, dst_ref=target, send_sem=send, recv_sem=recv,
+            device_id=peer, device_id_type=MESH,
+        )
+
+    def slot_at(way, dist):
+        return SLOT_OF[dist] if way == 0 else SLOT_OF[(n_z - dist) % n_z]
+
     def ring(way, n):
         dist, t = RING[way][n]
-        source = SLOT_OF[dist - 1] if way == 0 else SLOT_OF[(n_z - dist + 1) % n_z]
-        target = SLOT_OF[dist] if way == 0 else SLOT_OF[n_z - dist]
-        return pltpu.make_async_remote_copy(
-            src_ref=raw.at[t, pl.ds(source * chip, tok), :],
-            dst_ref=raw.at[t, pl.ds(target * chip, tok), :],
-            send_sem=ring_send.at[way, n],
-            recv_sem=ring_recv.at[way, n],
-            device_id=device(1 if way == 0 else n_z - 1, 0),
-            device_id_type=MESH,
+        return remote(
+            raw.at[t, pl.ds(slot_at(way, dist - 1) * chip, tok), :],
+            raw.at[t, pl.ds(slot_at(way, dist) * chip, tok), :],
+            ring_send.at[way, n],
+            ring_recv.at[way, n],
+            plane(1 if way == 0 else n_z - 1),
         )
 
     def sib(way, n):
-        if n < 0:
-            slot, t, index = 0, way, 7
-        else:
-            dist, t = RING[way][n]
-            slot, index = (SLOT_OF[dist] if way == 0 else SLOT_OF[n_z - dist]), n
-        return pltpu.make_async_remote_copy(
-            src_ref=raw.at[t, pl.ds(slot * chip, tok), :],
-            dst_ref=raw.at[t, pl.ds(slot * chip + tok, tok), :],
-            send_sem=sib_send.at[way, index],
-            recv_sem=sib_recv.at[way, index],
-            device_id=device(0, 1),
-            device_id_type=MESH,
-        )
-
-    def label_copy(o, r):
-        return pltpu.make_async_remote_copy(
-            src_ref=labels,
-            dst_ref=lab.at[SLOT_OF[o], r],
-            send_sem=lab_send.at[o, r],
-            recv_sem=lab_recv.at[o, r],
-            device_id=device(o, r),
-            device_id_type=MESH,
-        )
-
-    def hidden_copy(o, r):
-        return pltpu.make_async_remote_copy(
-            src_ref=stage.at[other if r else core, lax.rem(z + o, n_z)],
-            dst_ref=hid.at[pl.ds(SLOT_OF[o] * chip + r * tok, tok), :],
-            send_sem=hid_send.at[o, r],
-            recv_sem=hid_recv.at[o, r],
-            device_id=device(o, r),
-            device_id_type=MESH,
-        )
-
-    def err_copy(t):
-        return pltpu.make_async_remote_copy(
-            src_ref=errs[t].at[0],
-            dst_ref=err.at[1],
-            send_sem=err_send,
-            recv_sem=err_recv,
-            device_id=device(0, 1),
-            device_id_type=MESH,
-        )
-
-    def err_local(t):
-        return pltpu.make_async_copy(errs[t].at[0], err.at[0], local_sem.at[2])
+        dist, t = RING[way][n] if n < 7 else (0, way)
+        rows = slot_at(way, dist) * chip
+        return remote(
+            raw.at[t, pl.ds(rows, tok), :],
+            raw.at[t, pl.ds(rows + tok, tok), :],
+            sib_send.at[way, n],
+            sib_recv.at[way, n],
+            sibling,
+        )
+
+    def lab_copy(o):
+        return remote(
+            lab.at[0], lab.at[SLOT_OF[o]], lab_send.at[o], lab_recv.at[o], plane(o)
+        )
+
+    def hid_copy(o):
+        return remote(
+            stage.at[lax.rem(z + o, n_z)], blocks.at[SLOT_OF[o]],
+            hid_send.at[o], hid_recv.at[o], plane(o),
+        )
+
+    def lab_near():
+        return remote(lab.at[0, 0], lab.at[0, 1], near_send.at[0], near_recv.at[0], sibling)
+
+    def hid_near(source):
+        return remote(source, pair.at[1], near_send.at[1], near_recv.at[1], sibling)
+
+    def err_near(source):
+        return remote(source.at[0], err.at[1], near_send.at[2], near_recv.at[2], sibling)
+
+    def hid_local(source):
+        return pltpu.make_async_copy(source, pair.at[0], local_sem.at[2])
+
+    def err_local(source):
+        return pltpu.make_async_copy(source.at[0], err.at[0], local_sem.at[3])
 
     def normalize(slot, cross, t):
         rows = pl.ds(slot * chip + cross * tok, tok)
@@ -138,98 +132,119 @@
         emb[t, rows, :] = (values * inverse).astype(jnp.bfloat16)
         row_info[rows, t : t + 1] = inverse
 
-    for way in range(2):
-        ring(way, 0).start()
-    for way in range(2):
-        ring(way, 1).start()
+    for n in range(2):
+        for way in range(2):
+            ring(way, n).start()
     for t in range(2):
-        sib(t, -1).start()
-    for o, r in partners:
-        label_copy(o, r).start()
+        sib(t, 7).start()
+    lab[0, 0] = jnp.zeros(lab.shape[2:], jnp.float32)
+    lab[0, 0, :, 0:tok] = jnp.broadcast_to(labels[...].astype(jnp.float32), (8, tok))
+    lab_near().start()
 
     @pl.when(core == 0)
     def _():
-        err_copy(1).start()
-        err_local(0).start()
+        hid_near(hidden_b).start()
+        hid_local(hidden_a).start()
+        err_near(err_b).start()
+        err_local(err_a).start()
 
     @pl.when(core == 1)
     def _():
-        err_copy(0).start()
-        err_local(1).start()
-
-    lab[0, 0] = labels[...]
+        hid_near(hidden_a).start()
+        hid_local(hidden_b).start()
+        err_near(err_a).start()
+        err_local(err_b).start()
+
     row_sum[...] = jnp.zeros_like(row_sum)
     col_sum[...] = jnp.zeros_like(col_sum)
     for t in range(2):
         normalize(0, 0, t)
-    for t, hidden in enumerate((hidden_a, hidden_b)):
-        for k in range(n_z):
-            stage[t, k] = hidden[:, k * feat : (k + 1) * feat]
-
-    tile = 256
-
-    def tile_logits(r0, c0):
-        x = emb[core, pl.ds(r0, tile), :]
-        y = emb[other, pl.ds(c0, tile), :]
-        part = jnp.exp(
-            logit_scale * lax.dot_general(x, y, NT, preferred_element_type=jnp.float32)
-        )
-        logit[pl.ds(r0, tile), pl.ds(c0, tile)] = part
+    for t in range(2):
+        sib(t, 7).wait_recv()
+        normalize(0, 1, t)
+
+    def tile_logits(r0, c0, size):
+        x = emb[core, pl.ds(r0, size), :]
+        y = emb[other, pl.ds(c0, size), :]
+        part = jnp.exp2(
+            (logit_scale * LOG2E) * lax.dot_general(x, y, NT, preferred_element_type=jnp.float32)
+        )
+        logit[pl.ds(r0, size), pl.ds(c0, size)] = part
         lanes = part[:, 0:128]
-        for k in range(1, tile // 128):
+        for k in range(1, size // 128):
             lanes = lanes + part[:, k * 128 : (k + 1) * 128]
-        row_sum[pl.ds(r0, tile), :] += lanes
-        col_sum[:, pl.ds(c0, tile)] += jnp.sum(part.reshape(tile // 8, 8, tile), axis=0)
+        row_sum[pl.ds(r0, size), :] += lanes
+        col_sum[:, pl.ds(c0, size)] += jnp.sum(part.reshape(size // 8, 8, size), axis=0)
 
     def logits_to(old, new):
+        size = new - old
+
         def columns(k, _):
-            c0 = pl.multiple_of(old + (k // (new // tile)) * tile, tile)
-            r0 = pl.multiple_of(lax.rem(k, new // tile) * tile, tile)
-            tile_logits(r0, c0)
+            tile_logits(pl.multiple_of(k * size, 256), old, size)
             return 0
 
-        lax.fori_loop(0, ((new - old) // tile) * (new // tile), columns, 0)
+        def rows(k, _):
+            tile_logits(old, pl.multiple_of(k * size, 256), size)
+            return 0
+
+        lax.fori_loop(0, new // size, columns, 0)
         if old:
-
-            def rows(k, _):
-                c0 = pl.multiple_of((k // ((new - old) // tile)) * tile, tile)
-                r0 = pl.multiple_of(old + lax.rem(k, (new - old) // tile) * tile, tile)
-                tile_logits(r0, c0)
-                return 0
-
-            lax.fori_loop(0, ((new - old) // tile) * (old // tile), rows, 0)
+            lax.fori_loop(0, old // size, rows, 0)
+
+    wide = stage.shape[2]
+    narrow = feat - wide
+    part_rows = chip * narrow // wide
+
+    def pack():
+        for half in range(2):
+            for k in range(n_z):
+                first = k * feat
+                stage[k, half * tok : (half + 1) * tok, :] = pair[half, :, first : first + wide]
+                for g in range(tok // part_rows):
+                    lane = (half * (tok // part_rows) + g) * narrow
+                    stage[k, chip : chip + part_rows, lane : lane + narrow] = pair[
+                        half, g * part_rows : (g + 1) * part_rows, first + wide : first + feat
+                    ]
+
+    def unpack(slot, block):
+        rows = slot * chip
+        hid[rows : rows + chip, 0:wide] = block[0:chip, :]
+        for g in range(chip // part_rows):
+            hid[rows + g * part_rows : rows + (g + 1) * part_rows, wide:feat] = block[
+                chip : chip + part_rows, g * narrow : (g + 1) * narrow
+            ]
 
     last = len(RING[0])
-    bounds = [chip * k // tile * tile for k in (3, 5, 7)]
-    done = 0
+    bounds = (0, 768, 1536, 2048, group)
     for n in range(last):
         for way in range(2):
             ring(way, n).wait_recv()
             if n + 2 < last:
                 ring(way, n + 2).start()
             sib(way, n).start()
+        if n == last - 1:
+            for o in range(1, n_z):
+                lab_copy(o).start()
+            for o in range(1, n_z):
+                hid_copy(o).start()
         for way in range(2):
             dist, t = RING[way][n]
-            normalize(SLOT_OF[dist] if way == 0 else SLOT_OF[n_z - dist], 0, t)
-            sib(way, n - 1).wait_recv()
-            if n == 0:
-                normalize(0, 1, way)
-            else:
-                dist, t = RING[way][n - 1]
-                normalize(SLOT_OF[dist] if way == 0 else SLOT_OF[n_z - dist], 1, t)
-        if n == last - 1:
-            for o, r in partners:
-                hidden_copy(o, r).start()
-        if n in (2, 4, 6):
-            logits_to(done, bounds[n // 2 - 1])
-            done = bounds[n // 2 - 1]
-    for way in range(2):
-        sib(way, last - 1).wait_recv()
-        dist, t = RING[way][last - 1]
-        normalize(SLOT_OF[dist] if way == 0 else SLOT_OF[n_z - dist], 1, t)
-
-    for o, r in partners:
-        label_copy(o, r).wait_recv()
+            normalize(slot_at(way, dist), 0, t)
+        if n == 0:
+            hid_near(hidden_a).wait_recv()
+            hid_local(hidden_a).wait()
+            pack()
+            lab_near().wait_recv()
+        for way in range(2):
+            dist, t = RING[way][n]
+            sib(way, n).wait_recv()
+            normalize(slot_at(way, dist), 1, t)
+        if n % 2:
+            logits_to(bounds[n // 2], bounds[n // 2 + 1])
+    logits_to(bounds[3], bounds[4])
+
+    for o in range(1, n_z):
+        lab_copy(o).wait_recv()
     for slot in range(n_z):
         where = lax.rem(z + n_z - BEHIND[slot], n_z)
         for r in range(2):
@@ -244,8 +259,6 @@
         ids = row_info[k * 128 : (k + 1) * 128, 3:4]
         col_id[:, k * 128 : (k + 1) * 128] = jnp.broadcast_to(ids, (128, 128)).T[0:8, :]
 
-    logits_to(done, group)
-
     row_info[:, 4:5] = 0.5 / jnp.sum(row_sum[...], axis=1, keepdims=True)
     col_sum[0:1, :] = 0.5 / jnp.sum(col_sum[...], axis=0, keepdims=True)
     row_info[:, 5:6] = jnp.where(core == 0, row_info[:, 0:1], row_info[:, 1:2])
@@ -255,40 +268,31 @@
 
     def chunk_step(k, _):
         r0 = pl.multiple_of(k * chunk, chunk)
-
-        def weights(m, _):
-            rows = pl.ds(pl.multiple_of(r0 + m * fine, fine), fine)
-            base = row_info[rows, 4:5]
-            ids = row_info[rows, 2:3]
-            value = logit[rows, :] * (base + col_sum[0:1, :])
-            value = value - jnp.where(ids == col_id[0:1, :], 1.0, 0.0)
-            weight[pl.ds(pl.multiple_of(m * fine, fine), fine), :] = value.astype(jnp.bfloat16)
-            return 0
-
-        lax.fori_loop(0, chunk // fine, weights, 0)
+        for m in range(chunk // fine):
+            rows = pl.ds(r0 + m * fine, fine)
+            value = logit[rows, :] * (row_info[rows, 4:5] + col_sum[0:1, :])
+            value = value - jnp.where(row_info[rows, 2:3] == col_id[0:1, :], 1.0, 0.0)
+            weight[m * fine : (m + 1) * fine, :] = value.astype(jnp.bfloat16)
         grad[...] = lax.dot_general(
             weight[...], emb[other], NN, preferred_element_type=jnp.float32
         )
-
-        def finish(m, _):
-            rows = pl.ds(pl.multiple_of(r0 + m * fine, fine), fine)
+        for m in range(chunk // fine):
+            rows = pl.ds(r0 + m * fine, fine)
             inverse = row_info[rows, 5:6]
             unit = raw[core, rows, :].astype(jnp.float32) * inverse
-            value = logit_scale * grad[pl.ds(pl.multiple_of(m * fine, fine), fine), :]
+            value = logit_scale * grad[m * fine : (m + 1) * fine, :]
             along = jnp.sum(unit * value, axis=1, keepdims=True)
             emb[core, rows, :] = ((value - unit * along) * inverse).astype(jnp.bfloat16)
-            return 0
-
-        lax.fori_loop(0, chunk // fine, finish, 0)
         return 0
 
     lax.fori_loop(0, group // chunk, chunk_step, 0)
 
-    hid[0:tok, :] = stage[core, z]
-    for o, r in partners:
-        hidden_copy(o, r).wait_recv()
-    err_copy(0).wait_recv()
-    err_local(0).wait()
+    unpack(0, stage.at[z])
+    for o in range(1, n_z):
+        hid_copy(o).wait_recv()
+        unpack(SLOT_OF[o], blocks.at[SLOT_OF[o]])
+    err_near(err_a).wait_recv()
+    err_local(err_a).wait()
     total = lax.dot_general(hid[...], emb[core], TN, preferred_element_type=jnp.float32)
     for k in range(2):
         rows = slice(k * slab, (k + 1) * slab)
@@ -297,12 +301,14 @@
     for way in range(2):
         for n in range(last):
             ring(way, n).wait_send()
+        for n in range(last + 1):
             sib(way, n).wait_send()
-        sib(way, -1).wait_send()
-    for o, r in partners:
-        label_copy(o, r).wait_send()
-        hidden_copy(o, r).wait_send()
-    err_copy(0).wait_send()
+    for o in range(1, n_z):
+        lab_copy(o).wait_send()
+        hid_copy(o).wait_send()
+    lab_near().wait_send()
+    hid_near(hidden_a).wait_send()
+    err_near(err_a).wait_send()
 
 
 def head_gradient(n_z, proj_a, proj_b, labels, hidden_a, hidden_b, err_a, err_b):
@@ -310,15 +316,15 @@
     group = tok * n_z * 2
     feat = hidden_a.shape[1] // n_z
     slab = err_a.shape[1]
-    wide = labels.shape[1]
     chunk = 256
+    packed = 2 * tok * feat // 128
     dma = pltpu.SemaphoreType.DMA
     any_space = pl.BlockSpec(memory_space=pl.ANY)
     vmem = pl.BlockSpec(memory_space=pltpu.VMEM)
     return pl.pallas_call(
         functools.partial(grads_kernel, n_z),
         out_shape=jax.ShapeDtypeStruct((feat, width), jnp.float32),
-        in_specs=[any_space, any_space, vmem, vmem, vmem, any_space, any_space],
+        in_specs=[any_space, any_space, vmem] + [any_space] * 4,
         out_specs=vmem,
         scratch_shapes=[
             pltpu.VMEM((2, group, width), jnp.bfloat16),
@@ -330,21 +336,23 @@
             pltpu.VMEM((8, group), jnp.float32),
             pltpu.VMEM((group, 128), jnp.float32),
             pltpu.VMEM((8, group), jnp.float32),
-            pltpu.VMEM((n_z, 2, 8, wide), jnp.float32),
-            pltpu.VMEM((2, n_z, tok, feat), jnp.bfloat16),
+            pltpu.VMEM((n_z, 2, 8, 256), jnp.float32),
+            pltpu.VMEM((2, tok, feat * n_z), jnp.bfloat16),
+            pltpu.VMEM((n_z, packed, 128), jnp.bfloat16),
+            pltpu.VMEM((n_z, packed, 128), jnp.bfloat16),
             pltpu.VMEM((group, feat), jnp.bfloat16),
             pltpu.VMEM((2, slab, width), jnp.float32),
             dma((2, 7)),
             dma((2, 7)),
             dma((2, 8)),
             dma((2, 8)),
-            dma((n_z, 2)),
-            dma((n_z, 2)),
-            dma((n_z, 2)),
-            dma((n_z, 2)),
-            dma,
-            dma,
+            dma((n_z,)),
+            dma((n_z,)),
+            dma((n_z,)),
+            dma((n_z,)),
             dma((3,)),
+            dma((3,)),
+            dma((4,)),
         ],
         compiler_params=pltpu.CompilerParams(
             collective_id=0, has_side_effects=True, vmem_limit_bytes=63 * 1024 * 1024
@@ -561,11 +569,8 @@
 ):
     n_z = 8
     n_y = n_x = 4
-    tok = labels.shape[1]
-    wide = -(-tok // 128) * 128
-    spread = jnp.pad(labels.astype(jnp.float32), ((0, 7), (0, wide - tok)))
     mem = head_gradient(
-        n_z, audio_proj, score_proj, spread, audio_hidden, score_hidden, err_audio, err_score
+        n_z, audio_proj, score_proj, labels, audio_hidden, score_hidden, err_audio, err_score
     )
     p, q, new = compress(n_y, n_x, n_z, mem, q_seed)
     return (p[0], q[0], new[0:1], p[1], q[1], new[1:2])

time: 199 us -> 140 us (0.70)
  Pallas kernels: 190 us -> 133 us
    pallas_call x1, Pallas kernels: 152 us -> 92.3 us  [head_gradient(): pl.pallas_call(functools.partial(grads_kernel, n_z), out_shape=jax.ShapeD...]
where the time goes in v2:
time: 140 us
  Pallas kernels  133 us (95%)
  local copies, waits for them, and re-layouts  6.35 us (5%)
    pallas_call x1, Pallas kernels, head_gradient(): pl.pallas_call(functools.partial(grads_kernel, n_z), out_shape=jax.ShapeD...  92.3 us
    pallas_call x1, Pallas kernels, compress(): pl.pallas_call(functools.partial(compress_kernel, n_y, n_x, n_z), out_sha...  40.2 us
    unnamed x7, local copies, waits for them, and re-layouts  5.39 us

profile of v2, /device:TPU:1, one launch (start us, length us, event | category | flops | bytes accessed | tf_op | source)
XLA Modules:
  0.0 139.6 jit_solution(17673387759228966289)
XLA Ops:
  0.6 1.1 copy.14.seed
  1.8 92.3 %head_gradient.1.mem = f32[160,1024]{1,0:T(8,128)} custom-call(bf16[160,1024]{1,0:T(8,128)(2,1)} %proj_a.1, bf16[160,1024]{1,0:T(8,128)(2,1)} %proj_b.1, s32[1,160]{1,0:T(1,128)} %labels.1, bf16[160,1280]{1,0:T(8,128)(2,1)} %hidden_a.1, bf16[160,1280]{1,0:T(8,128)(2,1)} %hidden_b.1, f32[1,80,1024]{2,1,0:T(8,128)} %err_a.1, f32[1,80,1024]{2,1,0:T(8,128)} %err_b.1), custom_call_target="tpu_custom_call" | custom-call | tf_op jit(solution)/shard_map/head_gradient/pallas_call | solution.py:324
  94.1 0.0 copy-start
  94.1 1.1 copy-done
  95.2 40.2 %compress.1 = (f32[2,80,64]{2,1,0:T(8,128)S(1)}, f32[2,1024,64]{2,1,0:T(8,128)S(1)}, f32[2,80,1024]{2,1,0:T(8,128)S(1)}) custom-call(f32[160,1024]{1,0:T(8,128)S(1)} %copy-done, f32[1024,64]{1,0:T(8,128)S(1)} %copy.14.seed), custom_call_target="tpu_custom_call" | custom-call | tf_op jit(solution)/shard_map/compress/pallas_call | solution.py:528
  135.5 0.7 copy.17
  136.2 0.7 copy.15
  136.8 0.9 fusion
  137.7 0.1 slice_bitcast_fusion
  137.8 0.9 copy.18
  138.7 0.9 copy.16
  (1 shorter events, 0.0 us)
Async XLA Ops:
  94.1 1.1 copy-start

commit v3 on v2

v3 whole, which is shorter than its diff:
```python
import functools

import jax
import jax.numpy as jnp
from jax import lax
from jax.experimental import pallas as pl
from jax.experimental.pallas import tpu as pltpu
from jax.sharding import PartitionSpec as P

MESH = pl.DeviceIdType.MESH
logit_scale = 30.0
NORM_EPS = 1e-06
LOG2E = 1.4426950408889634
NT = (((1,), (1,)), ((), ()))
TN = (((0,), (0,)), ((), ()))
NN = (((1,), (0,)), ((), ()))
HIGH = lax.Precision.HIGHEST

SLOT_OF = (0, 1, 3, 5, 7, 6, 4, 2)
BEHIND = (0, 1, 7, 2, 6, 3, 5, 4)
RING = (
    ((1, 0), (1, 1), (2, 0), (2, 1), (3, 0), (3, 1), (4, 0)),
    ((1, 1), (1, 0), (2, 1), (2, 0), (3, 1), (3, 0), (4, 1)),
)


def exact(left, right, dims):
    return lax.dot_general(
        left, right, dims, precision=HIGH, preferred_element_type=jnp.float32
    )


BOUNDS = ((0, 0), (960, 768), (1600, 1536), (2240, 2048), (2560, 2560))
ROW_TILE = (480, 400, 560, 640)


def whole_kernel(
    n_y, n_x, n_z, proj_a, proj_b, labels, hidden_a, hidden_b, err_a, err_b, seed,
    p_ref, q_ref, new_ref,
    raw, emb, logit, weight, grad, row_sum, col_sum, row_info, col_id, lab, pair, stage, blocks,
    hid, err, mem, mem_sib, x_buf, y_buf, g_buf, part, gathered, z_buf, full, full_sib,
    coeff, resid, basis, basis_sib, p_own, p_sib,
    ring_send, ring_recv, sib_send, sib_recv, lab_send, lab_recv, hid_send, hid_recv,
    near_send, near_recv, local_sem,
    x_send, x_recv, y_send, y_recv, g_send, g_recv, r_send, r_recv, z_send, z_recv,
    f_send, f_recv, pair_send, pair_recv,
):
    n_rep = n_y * n_x
    rank, width = seed.shape
    tok = proj_a.shape[0]
    chip = 2 * tok
    group = raw.shape[1]
    feat = hid.shape[1]
    slab = err_a.shape[1]
    rep = lax.axis_index("rep")
    con = lax.axis_index("con")
    y = rep // n_x
    x = lax.rem(rep, n_x)
    z = con // 2
    core = lax.rem(con, 2)
    other = 1 - core

    def plane(ahead):
        return (rep, lax.rem(z + ahead, n_z) * 2 + core)

    sibling = (rep, z * 2 + other)

    def along_x(i):
        return (y * n_x + lax.rem(x + i, n_x), con)

    def along_y(i):
        return (lax.rem(y + i, n_y) * n_x + x, con)

    def along_rep(i):
        return (lax.rem(rep + i, n_rep), con)

    projs = (proj_a, proj_b)
    loads = [
        pltpu.make_async_copy(projs[t], raw.at[t, pl.ds(0, tok), :], local_sem.at[t])
        for t in range(2)
    ]
    for load in loads:
        load.start()

    lab[0, 0] = jnp.zeros(lab.shape[2:], jnp.float32)
    lab[0, 0, :, 0:tok] = jnp.broadcast_to(labels[...].astype(jnp.float32), (8, tok))

    barrier = pltpu.get_barrier_semaphore()
    greet = [plane(1), plane(n_z - 1), sibling]
    greet += [along_x(i) for i in range(1, n_x)] + [along_y(i) for i in range(1, n_y)]
    for peer in greet:
        pl.semaphore_signal(barrier, inc=1, device_id=peer, device_id_type=MESH)
    pl.semaphore_wait(barrier, len(greet))
    for load in loads:
        load.wait()

    def remote(source, target, send, recv, peer):
        return pltpu.make_async_remote_copy(
            src_ref=source, dst_ref=target, send_sem=send, recv_sem=recv,
            device_id=peer, device_id_type=MESH,
        )

    def slot_at(way, dist):
        return SLOT_OF[dist] if way == 0 else SLOT_OF[(n_z - dist) % n_z]

    def ring(way, n):
        dist, t = RING[way][n]
        return remote(
            raw.at[t, pl.ds(slot_at(way, dist - 1) * chip, tok), :],
            raw.at[t, pl.ds(slot_at(way, dist) * chip, tok), :],
            ring_send.at[way, n],
            ring_recv.at[way, n],
            plane(1 if way == 0 else n_z - 1),
        )

    def sib(way, n):
        dist, t = RING[way][n] if n < 7 else (0, way)
        rows = slot_at(way, dist) * chip
        return remote(
            raw.at[t, pl.ds(rows, tok), :],
            raw.at[t, pl.ds(rows + tok, tok), :],
            sib_send.at[way, n],
            sib_recv.at[way, n],
            sibling,
        )

    def lab_copy(way, dist):
        return remote(
            lab.at[0, slot_at(way, dist - 1)], lab.at[0, slot_at(way, dist)],
            lab_send.at[way, dist - 1], lab_recv.at[way, dist - 1],
            plane(1 if way == 0 else n_z - 1),
        )

    def hid_copy(o):
        return remote(
            stage.at[lax.rem(z + o, n_z)], blocks.at[SLOT_OF[o]],
            hid_send.at[o], hid_recv.at[o], plane(o),
        )

    def lab_near():
        return remote(lab.at[0], lab.at[1], near_send.at[0], near_recv.at[0], sibling)

    def hid_near(source):
        return remote(source, pair.at[1], near_send.at[1], near_recv.at[1], sibling)

    def err_near(source):
        return remote(source.at[0], err.at[1], near_send.at[2], near_recv.at[2], sibling)

    def hid_local(source):
        return pltpu.make_async_copy(source, pair.at[0], local_sem.at[2])

    def err_local(source):
        return pltpu.make_async_copy(source.at[0], err.at[0], local_sem.at[3])

    def normalize(slot, cross, t):
        rows = pl.ds(slot * chip + cross * tok, tok)
        values = raw[t, rows, :].astype(jnp.float32)
        inverse = lax.rsqrt(jnp.sum(values * values, axis=1, keepdims=True) + NORM_EPS)
        emb[t, rows, :] = (values * inverse).astype(jnp.bfloat16)
        row_info[rows, t : t + 1] = inverse

    for way in range(2):
        lab_copy(way, 1).start()
    for n in range(2):
        for way in range(2):
            ring(way, n).start()
    for t in range(2):
        sib(t, 7).start()

    @pl.when(core == 0)
    def _():
        hid_near(hidden_b).start()
        hid_local(hidden_a).start()
        err_near(err_b).start()
        err_local(err_a).start()

    @pl.when(core == 1)
    def _():
        hid_near(hidden_a).start()
        hid_local(hidden_b).start()
        err_near(err_a).start()
        err_local(err_b).start()

    row_sum[...] = jnp.zeros_like(row_sum)
    col_sum[...] = jnp.zeros_like(col_sum)
    for t in range(2):
        normalize(0, 0, t)
    for t in range(2):
        sib(t, 7).wait_recv()
        normalize(0, 1, t)

    def tile_logits(r0, rows, c0, cols):
        left = emb[core, pl.ds(r0, rows), :]
        right = emb[other, pl.ds(c0, cols), :]
        part = jnp.exp2(
            (logit_scale * LOG2E)
            * lax.dot_general(left, right, NT, preferred_element_type=jnp.float32)
        )
        logit[pl.ds(r0, rows), pl.ds(c0, cols)] = part
        lanes = part[:, 0:128]
        for k in range(1, cols // 128):
            lanes = lanes + part[:, k * 128 : (k + 1) * 128]
        row_sum[pl.ds(r0, rows), :] += lanes
        col_sum[:, pl.ds(c0, cols)] += jnp.sum(part.reshape(rows // 8, 8, cols), axis=0)

    def logits_step(step):
        old_rows, old_cols = BOUNDS[step]
        new_rows, new_cols = BOUNDS[step + 1]
        cols = new_cols - old_cols
        rows = ROW_TILE[step]

        def columns(k, _):
            tile_logits(pl.multiple_of(k * rows, 16), rows, old_cols, cols)
            return 0

        lax.fori_loop(0, new_rows // rows, columns, 0)
        if old_cols:
            cut = 768 if step == 1 else 512

            def more(k, _):
                tile_logits(old_rows, new_rows - old_rows, pl.multiple_of(k * cut, 256), cut)
                return 0

            lax.fori_loop(0, old_cols // cut, more, 0)

    wide = stage.shape[2]
    narrow = feat - wide
    part_rows = chip * narrow // wide

    def pack():
        for half in range(2):
            for k in range(n_z):
                first = k * feat
                stage[k, half * tok : (half + 1) * tok, :] = pair[half, :, first : first + wide]
                for g in range(tok // part_rows):
                    lane = (half * (tok // part_rows) + g) * narrow
                    stage[k, chip : chip + part_rows, lane : lane + narrow] = pair[
                        half, g * part_rows : (g + 1) * part_rows, first + wide : first + feat
                    ]

    def unpack(slot, block):
        rows = slot * chip
        hid[rows : rows + chip, 0:wide] = block[0:chip, :]
        for g in range(chip // part_rows):
            hid[rows + g * part_rows : rows + (g + 1) * part_rows, wide:feat] = block[
                chip : chip + part_rows, g * narrow : (g + 1) * narrow
            ]

    def pair_ids():
        for slot in range(n_z):
            where = lax.rem(z + n_z - BEHIND[slot], n_z)
            for r in range(2):
                first = ((where * 2 + (other if r else core)) * tok).astype(jnp.float32)
                piece = lab[r, slot]
                spread = jnp.broadcast_to(piece[0:1, :], (128, piece.shape[1])).T[:tok, 0:1]
                own = first + lax.broadcasted_iota(jnp.int32, (tok, 1), 0).astype(jnp.float32)
                rows = pl.ds(slot * chip + r * tok, tok)
                row_info[rows, 2:3] = jnp.where(core == 0, spread, own)
                row_info[rows, 3:4] = jnp.where(core == 0, own, spread)
        for k in range(group // 128):
            ids = row_info[k * 128 : (k + 1) * 128, 3:4]
            col_id[:, k * 128 : (k + 1) * 128] = jnp.broadcast_to(ids, (128, 128)).T[0:8, :]

    last = len(RING[0])
    for n in range(last):
        for way in range(2):
            ring(way, n).wait_recv()
            if n < (4, 3)[way]:
                lab_copy(way, n + 1).wait_recv()
            if n + 2 <= (4, 3)[way]:
                lab_copy(way, n + 2).start()
            if n + 2 < last:
                ring(way, n + 2).start()
            sib(way, n).start()
        if n == last - 1:
            for o in range(1, n_z):
                hid_copy(o).start()
        for way in range(2):
            dist, t = RING[way][n]
            normalize(slot_at(way, dist), 0, t)
        if n == 0:
            hid_near(hidden_a).wait_recv()
            hid_local(hidden_a).wait()
            pack()
        if n == 3:
            lab_near().start()
        for way in range(2):
            dist, t = RING[way][n]
            sib(way, n).wait_recv()
            normalize(slot_at(way, dist), 1, t)
        if n % 2:
            logits_step(n // 2)
        if n == 4:
            lab_near().wait_recv()
            pair_ids()
    logits_step(3)

    row_info[:, 4:5] = 0.5 / jnp.sum(row_sum[...], axis=1, keepdims=True)
    col_sum[0:1, :] = 0.5 / jnp.sum(col_sum[...], axis=0, keepdims=True)
    row_info[:, 5:6] = jnp.where(core == 0, row_info[:, 0:1], row_info[:, 1:2])

    chunk = weight.shape[0]
    fine = 16

    def chunk_step(k, _):
        r0 = pl.multiple_of(k * chunk, chunk)
        for m in range(chunk // fine):
            rows = pl.ds(r0 + m * fine, fine)
            value = logit[rows, :] * (row_info[rows, 4:5] + col_sum[0:1, :])
            value = value - jnp.where(row_info[rows, 2:3] == col_id[0:1, :], 1.0, 0.0)
            weight[m * fine : (m + 1) * fine, :] = value.astype(jnp.bfloat16)
        grad[...] = lax.dot_general(
            weight[...], emb[other], NN, preferred_element_type=jnp.float32
        )
        for m in range(chunk // fine):
            rows = pl.ds(r0 + m * fine, fine)
            inverse = row_info[rows, 5:6]
            unit = raw[core, rows, :].astype(jnp.float32) * inverse
            value = logit_scale * grad[m * fine : (m + 1) * fine, :]
            along = jnp.sum(unit * value, axis=1, keepdims=True)
            emb[core, rows, :] = ((value - unit * along) * inverse).astype(jnp.bfloat16)
        return 0

    lax.fori_loop(0, group // chunk, chunk_step, 0)

    unpack(0, stage.at[z])
    for o in range(1, n_z):
        hid_copy(o).wait_recv()
        unpack(SLOT_OF[o], blocks.at[SLOT_OF[o]])
    err_near(err_a).wait_recv()
    err_local(err_a).wait()
    total = lax.dot_general(hid[...], emb[core], TN, preferred_element_type=jnp.float32)
    for k in range(2):
        rows = slice(k * slab, (k + 1) * slab)
        mem[rows, :] = total[rows, :] + err[jnp.where(core == k, 0, 1)]

    theirs = pl.ds(pl.multiple_of(other * slab, 8), slab)
    ours = pl.ds(pl.multiple_of(core * slab, 8), slab)
    mem_copy = remote(mem.at[theirs, :], mem_sib, pair_send.at[0], pair_recv.at[0], sibling)
    mem_copy.start()

    def all_sum(buf, index, count, send, recv, peers, value):
        buf[index] = value
        copies = [
            remote(buf.at[index], buf.at[index], send.at[i], recv.at[i], peers(i))
            for i in range(1, count)
        ]
        for one in copies:
            one.start()

        def finish():
            for one in copies:
                one.wait()
            total = buf[0]
            for k in range(1, count):
                total = total + buf[k]
            return total

        return finish

    left = exact(seed[...], mem[...], NT)
    strip = rank // 4
    packed = jnp.concatenate(
        [left[:, :128]]
        + [jnp.concatenate([left[g * strip : (g + 1) * strip, 128:] for g in range(4)], axis=1)],
        axis=0,
    )
    packed = all_sum(x_buf, x, n_x, x_send, x_recv, along_x, packed)()
    packed = all_sum(y_buf, y, n_y, y_send, y_recv, along_y, packed)()
    tail = [packed[rank:, g * 32 : (g + 1) * 32] for g in range(4)]
    left = jnp.concatenate([packed[:rank, :], jnp.concatenate(tail, axis=0)], axis=1)

    gram = exact(left, left, NT)
    gram_sum = all_sum(
        g_buf, z, n_z, g_send, g_recv, plane,
        jnp.concatenate([gram[: rank // 2, :], gram[rank // 2 :, :]], axis=1),
    )
    right = exact(left, mem[...], NN)
    span = width // 2
    for k in range(n_rep):
        part[k] = right[8 * (k // 2) : 8 * (k // 2) + 8, span * (k % 2) : span * (k % 2) + span]
    gathered[rep] = part[rep]
    reduce = [
        remote(
            part.at[lax.rem(rep + i, n_rep)], gathered.at[rep], r_send.at[i], r_recv.at[i],
            along_rep(i),
        )
        for i in range(1, n_rep)
    ]
    for one in reduce:
        one.start()

    gram = gram_sum()
    resid[...] = jnp.concatenate([gram[:, :rank], gram[:, rank:]], axis=0)
    coeff[...] = (
        lax.broadcasted_iota(jnp.int32, (rank, rank), 0)
        == lax.broadcasted_iota(jnp.int32, (rank, rank), 1)
    ).astype(jnp.float32)

    def column_step(k, _):
        lane = lax.broadcasted_iota(jnp.int32, (rank, rank), 1)
        u = coeff[pl.ds(k, 1), :]
        w = resid[pl.ds(k, 1), :]
        values = resid[...]
        square = jnp.maximum(jnp.sum(u * w, axis=1, keepdims=True), 0.0) + NORM_EPS
        column = jnp.sum(jnp.where(lane == k, values, 0.0), axis=1, keepdims=True)
        inverse = 1.0 / square
        basis[pl.ds(k, 1), :] = u * lax.rsqrt(square)
        coeff[...] -= column * (u * inverse)
        resid[...] = values - column * (w * inverse)
        return 0

    cuts = [0, rank // 3, 2 * rank // 3, rank]
    lax.fori_loop(cuts[0], cuts[1], column_step, 0)
    for one in reduce:
        one.wait()
    total = gathered[0]
    for k in range(1, n_rep):
        total = total + gathered[k]
    z_sum = all_sum(z_buf, z, n_z, z_send, z_recv, plane, total)
    lax.fori_loop(cuts[1], cuts[2], column_step, 0)
    full[rep] = z_sum()
    spread = [
        remote(full.at[rep], full.at[rep], f_send.at[i], f_recv.at[i], along_rep(i))
        for i in range(1, n_rep)
    ]
    for one in spread:
        one.start()
    lax.fori_loop(cuts[2], cuts[3], column_step, 0)

    turn_copy = remote(basis, basis_sib, pair_send.at[2], pair_recv.at[2], sibling)
    turn_copy.start()
    turn = basis[...]
    factor = exact(turn, left, NN)
    for k in range(2):
        p_own[k] = factor[:, k * slab : (k + 1) * slab]
    p_copy = remote(p_own.at[other], p_sib, pair_send.at[1], pair_recv.at[1], sibling)
    p_copy.start()
    for one in spread:
        one.wait_recv()
    full_copy = remote(full, full_sib, pair_send.at[3], pair_recv.at[3], sibling)
    full_copy.start()

    def finish(head, turn, blocks, memory, factor):
        right = jnp.concatenate(
            [
                jnp.concatenate([blocks[2 * k], blocks[2 * k + 1]], axis=1)
                for k in range(n_rep // 2)
            ],
            axis=0,
        )
        right = exact(turn, right, NN) / n_rep
        q_ref[head] = right
        p_ref[head] = factor
        new_ref[head] = memory - exact(factor, right, TN)

    finish(core, turn, full, mem[ours, :], p_own[core])
    mem_copy.wait()
    p_copy.wait()
    turn_copy.wait()
    full_copy.wait()
    finish(other, basis_sib[...], full_sib, mem_sib[...], p_sib[...])
    for one in spread:
        one.wait_send()

    for way in range(2):
        for n in range(last):
            ring(way, n).wait_send()
        for n in range(last + 1):
            sib(way, n).wait_send()
        for dist in range(1, (5, 4)[way]):
            lab_copy(way, dist).wait_send()
    for o in range(1, n_z):
        hid_copy(o).wait_send()
    lab_near().wait_send()
    hid_near(hidden_a).wait_send()
    err_near(err_a).wait_send()


def whole(n_y, n_x, n_z, proj_a, proj_b, labels, hidden_a, hidden_b, err_a, err_b, seed):
    tok, width = proj_a.shape
    rank = seed.shape[0]
    group = tok * n_z * 2
    feat = hidden_a.shape[1] // n_z
    slab = err_a.shape[1]
    n_rep = n_y * n_x
    chunk = 256
    packed = 2 * tok * feat // 128
    dma = pltpu.SemaphoreType.DMA
    any_space = pl.BlockSpec(memory_space=pl.ANY)
    vmem = pl.BlockSpec(memory_space=pltpu.VMEM)
    f32 = jnp.float32
    return pl.pallas_call(
        functools.partial(whole_kernel, n_y, n_x, n_z),
        out_shape=(
            jax.ShapeDtypeStruct((2, rank, slab), f32),
            jax.ShapeDtypeStruct((2, rank, width), f32),
            jax.ShapeDtypeStruct((2, slab, width), f32),
        ),
        in_specs=[any_space, any_space, vmem] + [any_space] * 4 + [vmem],
        out_specs=[vmem] * 3,
        scratch_shapes=[
            pltpu.VMEM((2, group, width), jnp.bfloat16),
            pltpu.VMEM((2, group, width), jnp.bfloat16),
            pltpu.VMEM((group, group), f32),
            pltpu.VMEM((chunk, group), jnp.bfloat16),
            pltpu.VMEM((chunk, width), f32),
            pltpu.VMEM((group, 128), f32),
            pltpu.VMEM((8, group), f32),
            pltpu.VMEM((group, 128), f32),
            pltpu.VMEM((8, group), f32),
            pltpu.VMEM((2, n_z, 8, 256), f32),
            pltpu.VMEM((2, tok, feat * n_z), jnp.bfloat16),
            pltpu.VMEM((n_z, packed, 128), jnp.bfloat16),
            pltpu.VMEM((n_z, packed, 128), jnp.bfloat16),
            pltpu.VMEM((group, feat), jnp.bfloat16),
            pltpu.VMEM((2, slab, width), f32),
            pltpu.VMEM((feat, width), f32),
            pltpu.VMEM((slab, width), f32),
            pltpu.VMEM((n_x, slab, 2 * rank), f32),
            pltpu.VMEM((n_y, slab, 2 * rank), f32),
            pltpu.VMEM((n_z, rank // 2, 2 * rank), f32),
            pltpu.VMEM((n_rep, 8, width // 2), f32),
            pltpu.VMEM((n_rep, 8, width // 2), f32),
            pltpu.VMEM((n_z, 8, width // 2), f32),
            pltpu.VMEM((n_rep, 8, width // 2), f32),
            pltpu.VMEM((n_rep, 8, width // 2), f32),
            pltpu.VMEM((rank, rank), f32),
            pltpu.VMEM((rank, rank), f32),
            pltpu.VMEM((rank, rank), f32),
            pltpu.VMEM((rank, rank), f32),
            pltpu.VMEM((2, rank, slab), f32),
            pltpu.VMEM((rank, slab), f32),
            dma((2, 7)), dma((2, 7)),
            dma((2, 8)), dma((2, 8)),
            dma((2, 4)), dma((2, 4)),
            dma((n_z,)), dma((n_z,)),
            dma((3,)), dma((3,)),
            dma((4,)),
            dma((n_x,)), dma((n_x,)),
            dma((n_y,)), dma((n_y,)),
            dma((n_z,)), dma((n_z,)),
            dma((n_rep,)), dma((n_rep,)),
            dma((n_z,)), dma((n_z,)),
            dma((n_rep,)), dma((n_rep,)),
            dma((4,)), dma((4,)),
        ],
        compiler_params=pltpu.CompilerParams(
            collective_id=0, has_side_effects=True, vmem_limit_bytes=63 * 1024 * 1024
        ),
        name="whole",
    )(proj_a, proj_b, labels, hidden_a, hidden_b, err_a, err_b, seed)


def shards(
    audio_hidden, score_hidden, audio_proj, score_proj, labels, q_seed, err_audio, err_score
):
    n_z = 8
    n_y = n_x = 4
    p, q, new = whole(
        n_y, n_x, n_z, audio_proj, score_proj, labels, audio_hidden, score_hidden,
        err_audio, err_score, q_seed.T,
    )
    return (p[0].T, q[0].T, new[0:1], p[1].T, q[1].T, new[1:2])


def solution(mesh):
    placed = (
        P(("rep", "con"), None),
        P(("rep", "con"), None),
        P(("rep", "con"), None),
        P(("rep", "con"), None),
        P("rep", "con"),
        P(),
        P("rep", "con", None),
        P("rep", "con", None),
    )
    return jax.shard_map(
        shards,
        mesh=mesh,
        in_specs=placed,
        out_specs=(
            P("con", None),
            P(),
            P("rep", "con", None),
            P("con", None),
            P(),
            P("rep", "con", None),
        ),
        check_vma=False,
    )
```

time: 140 us -> 132 us (0.943)
  Pallas kernels: 133 us -> 127 us
  local copies, waits for them, and re-layouts: 6.35 us -> 4.22 us
    pallas_call x2 -> x1, Pallas kernels: 133 us -> 127 us  [whole(): pl.pallas_call(functools.partial(whole_kernel, n_y, n_x, n_z), out_shape=...]
    unnamed x7 -> x2, local copies, waits for them, and re-layouts: 5.39 us -> 0.01 us
    transpose x0 -> x2, local copies, waits for them, and re-layouts: none -> 3.34 us  [shards(): return (p[0].T, q[0].T, new[0:1], p[1].T, q[1].T, new[1:2])]
where the time goes in v3:
time: 132 us
  Pallas kernels  127 us (96%)
  local copies, waits for them, and re-layouts  4.22 us (3%)
    pallas_call x1, Pallas kernels, whole(): pl.pallas_call(functools.partial(whole_kernel, n_y, n_x, n_z), out_shape=...  127 us
    transpose x2, local copies, waits for them, and re-layouts, shards(): return (p[0].T, q[0].T, new[0:1], p[1].T, q[1].T, new[1:2])  3.34 us

profile of v3, /device:TPU:1, one launch (start us, length us, event | category | flops | bytes accessed | tf_op | source)
XLA Modules:
  0.0 131.5 jit_solution(12499316520559446846)
XLA Ops:
  0.6 126.7 %whole.1 = (f32[2,64,80]{2,1,0:T(8,128)}, f32[2,64,1024]{2,1,0:T(8,128)}, f32[2,80,1024]{2,1,0:T(8,128)}) custom-call(bf16[160,1024]{1,0:T(8,128)(2,1)} %proj_a.1, bf16[160,1024]{1,0:T(8,128)(2,1)} %proj_b.1, s32[1,160]{1,0:T(1,128)} %labels.1, bf16[160,1280]{1,0:T(8,128)(2,1)} %hidden_a.1, bf16[160,1280]{1,0:T(8,128)(2,1)} %hidden_b.1, ...), custom_call_target="tpu_custom_call" | custom-call | tf_op jit(solution)/shard_map/whole/pallas_call | solution.py:493
  127.3 0.0 copy-start
  127.3 1.5 %slice_bitcast_fusion.2 = (f32[80,64]{0,1:T(8,128)}, f32[80,64]{0,1:T(8,128)}) fusion(f32[2,64,80]{2,1,0:T(8,128)} %get-tuple-element.9), kind=kLoop, calls=%fused_computation.2 | loop fusion | bytes 81920 | tf_op jit(solution)/shard_map/transpose | solution.py:564
  128.8 1.9 %slice_bitcast_fusion = (f32[1024,64]{0,1:T(8,128)}, f32[1024,64]{0,1:T(8,128)}) fusion(f32[2,64,1024]{2,1,0:T(8,128)} %get-tuple-element.10), kind=kLoop, calls=%fused_computation | loop fusion | bytes 1048576 | tf_op jit(solution)/shard_map/transpose | solution.py:564
  130.7 0.0 copy-done
  130.7 0.9 fusion
Async XLA Ops:
  127.3 3.3 %copy-start = (f32[2,80,1024]{2,1,0:T(8,128)S(1)}, f32[2,80,1024]{2,1,0:T(8,128)}, u32[]{:S(2)}) copy-start(f32[2,80,1024]{2,1,0:T(8,128)} %get-tuple-element.11) | copy-start | bytes 1966084

commit v4 on v3

--- a/solution.py
+++ b/solution.py
@@ -19,9 +19,10 @@
 SLOT_OF = (0, 1, 3, 5, 7, 6, 4, 2)
 BEHIND = (0, 1, 7, 2, 6, 3, 5, 4)
 RING = (
-    ((1, 0), (1, 1), (2, 0), (2, 1), (3, 0), (3, 1), (4, 0)),
-    ((1, 1), (1, 0), (2, 1), (2, 0), (3, 1), (3, 0), (4, 1)),
+    ((1, 0), (1, 1), (2, 0), (2, 1), (3, 0), (3, 1), (4, 0), (4, 0)),
+    ((1, 1), (1, 0), (2, 1), (2, 0), (3, 1), (3, 0), (4, 1), (4, 1)),
 )
+FAR = 7
 
 
 def exact(left, right, dims):
@@ -30,14 +31,17 @@
     )
 
 
-BOUNDS = ((0, 0), (960, 768), (1600, 1536), (2240, 2048), (2560, 2560))
-ROW_TILE = (480, 400, 560, 640)
+OWN = 8
+
+BOUNDS = ((0, 0), (960, 768), (1600, 1536), (2240, 2048), (2400, 2304), (2560, 2560))
+ROW_TILE = (480, 400, 560, 600, 640)
+COL_TILE = (0, 768, 512, 512, 768)
 
 
 def whole_kernel(
     n_y, n_x, n_z, proj_a, proj_b, labels, hidden_a, hidden_b, err_a, err_b, seed,
-    p_ref, q_ref, new_ref,
-    raw, emb, logit, weight, grad, row_sum, col_sum, row_info, col_id, lab, pair, stage, blocks,
+    p_ref, q_ref, mem_ref,
+    raw, emb, logit, weight, grad, col_sum, row_info, col_id, lab, pair, stage, blocks,
     hid, err, mem, mem_sib, x_buf, y_buf, g_buf, part, gathered, z_buf, full, full_sib,
     coeff, resid, basis, basis_sib, p_own, p_sib,
     ring_send, ring_recv, sib_send, sib_recv, lab_send, lab_recv, hid_send, hid_recv,
@@ -103,22 +107,36 @@
     def slot_at(way, dist):
         return SLOT_OF[dist] if way == 0 else SLOT_OF[(n_z - dist) % n_z]
 
+    half = tok // 2
+
+    def place(slot, cross, part):
+        if slot == FAR:
+            return slot * chip + (part * 2 + cross) * half, half
+        return slot * chip + cross * tok, tok
+
+    def item(way, n):
+        dist, t = RING[way][n]
+        return dist, t, slot_at(way, dist), (n - 6 if dist == 4 else 0)
+
     def ring(way, n):
-        dist, t = RING[way][n]
+        dist, t, slot, part = item(way, n)
+        first, rows = place(slot, 0, part)
+        source = place(slot_at(way, dist - 1), 0, 0)[0] + part * half
         return remote(
-            raw.at[t, pl.ds(slot_at(way, dist - 1) * chip, tok), :],
-            raw.at[t, pl.ds(slot_at(way, dist) * chip, tok), :],
+            raw.at[t, pl.ds(source, rows), :],
+            raw.at[t, pl.ds(first, rows), :],
             ring_send.at[way, n],
             ring_recv.at[way, n],
             plane(1 if way == 0 else n_z - 1),
         )
 
     def sib(way, n):
-        dist, t = RING[way][n] if n < 7 else (0, way)
-        rows = slot_at(way, dist) * chip
+        dist, t, slot, part = item(way, n) if n < OWN else (0, way, 0, 0)
+        first, rows = place(slot, 0, part)
+        target, _ = place(slot, 1, part)
         return remote(
-            raw.at[t, pl.ds(rows, tok), :],
-            raw.at[t, pl.ds(rows + tok, tok), :],
+            raw.at[t, pl.ds(first, rows), :],
+            raw.at[t, pl.ds(target, rows), :],
             sib_send.at[way, n],
             sib_recv.at[way, n],
             sibling,
@@ -152,8 +170,9 @@
     def err_local(source):
         return pltpu.make_async_copy(source.at[0], err.at[0], local_sem.at[3])
 
-    def normalize(slot, cross, t):
-        rows = pl.ds(slot * chip + cross * tok, tok)
+    def normalize(slot, cross, t, part=0):
+        first, count = place(slot, cross, part)
+        rows = pl.ds(first, count)
         values = raw[t, rows, :].astype(jnp.float32)
         inverse = lax.rsqrt(jnp.sum(values * values, axis=1, keepdims=True) + NORM_EPS)
         emb[t, rows, :] = (values * inverse).astype(jnp.bfloat16)
@@ -165,7 +184,7 @@
         for way in range(2):
             ring(way, n).start()
     for t in range(2):
-        sib(t, 7).start()
+        sib(t, OWN).start()
 
     @pl.when(core == 0)
     def _():
@@ -181,12 +200,12 @@
         err_near(err_a).start()
         err_local(err_b).start()
 
-    row_sum[...] = jnp.zeros_like(row_sum)
+    row_info[...] = jnp.zeros_like(row_info)
     col_sum[...] = jnp.zeros_like(col_sum)
     for t in range(2):
         normalize(0, 0, t)
     for t in range(2):
-        sib(t, 7).wait_recv()
+        sib(t, OWN).wait_recv()
         normalize(0, 1, t)
 
     def tile_logits(r0, rows, c0, cols):
@@ -200,7 +219,7 @@
         lanes = part[:, 0:128]
         for k in range(1, cols // 128):
             lanes = lanes + part[:, k * 128 : (k + 1) * 128]
-        row_sum[pl.ds(r0, rows), :] += lanes
+        row_info[pl.ds(r0, rows), 6:7] += jnp.sum(lanes, axis=1, keepdims=True)
         col_sum[:, pl.ds(c0, cols)] += jnp.sum(part.reshape(rows // 8, 8, cols), axis=0)
 
     def logits_step(step):
@@ -213,15 +232,28 @@
             tile_logits(pl.multiple_of(k * rows, 16), rows, old_cols, cols)
             return 0
 
-        lax.fori_loop(0, new_rows // rows, columns, 0)
-        if old_cols:
-            cut = 768 if step == 1 else 512
-
-            def more(k, _):
-                tile_logits(old_rows, new_rows - old_rows, pl.multiple_of(k * cut, 256), cut)
-                return 0
-
-            lax.fori_loop(0, old_cols // cut, more, 0)
+        def more(k, _):
+            first = pl.multiple_of(k * COL_TILE[step], 256)
+            tile_logits(old_rows, new_rows - old_rows, first, COL_TILE[step])
+            return 0
+
+        if step < 2:
+            lax.fori_loop(0, new_rows // rows, columns, 0)
+        else:
+            for k in range(new_rows // rows):
+                tile_logits(k * rows, rows, old_cols, cols)
+        if step == 2:
+            late_rows(other)
+        elif step == 1:
+            lax.fori_loop(0, old_cols // COL_TILE[step], more, 0)
+        elif old_cols:
+            for k in range(old_cols // COL_TILE[step]):
+                tile_logits(old_rows, new_rows - old_rows, k * COL_TILE[step], COL_TILE[step])
+
+    def late_rows(which):
+        first = pl.multiple_of(5 * chip + which * chip, 16)
+        for k in range(BOUNDS[2][1] // COL_TILE[2]):
+            tile_logits(first, chip, k * COL_TILE[2], COL_TILE[2])
 
     wide = stage.shape[2]
     narrow = feat - wide
@@ -239,10 +271,12 @@
                     ]
 
     def unpack(slot, block):
-        rows = slot * chip
-        hid[rows : rows + chip, 0:wide] = block[0:chip, :]
         for g in range(chip // part_rows):
-            hid[rows + g * part_rows : rows + (g + 1) * part_rows, wide:feat] = block[
+            cross, part = g // 2, g % 2
+            first = place(slot, cross, part)[0] + (0 if slot == FAR else part * half)
+            source = slice(g * part_rows, (g + 1) * part_rows)
+            hid[first : first + part_rows, 0:wide] = block[source, :]
+            hid[first : first + part_rows, wide:feat] = block[
                 chip : chip + part_rows, g * narrow : (g + 1) * narrow
             ]
 
@@ -254,9 +288,13 @@
                 piece = lab[r, slot]
                 spread = jnp.broadcast_to(piece[0:1, :], (128, piece.shape[1])).T[:tok, 0:1]
                 own = first + lax.broadcasted_iota(jnp.int32, (tok, 1), 0).astype(jnp.float32)
-                rows = pl.ds(slot * chip + r * tok, tok)
-                row_info[rows, 2:3] = jnp.where(core == 0, spread, own)
-                row_info[rows, 3:4] = jnp.where(core == 0, own, spread)
+                ids_row = jnp.where(core == 0, spread, own)
+                ids_col = jnp.where(core == 0, own, spread)
+                for part in range(2):
+                    start = place(slot, r, part)[0] + (0 if slot == FAR else part * half)
+                    source = slice(part * half, (part + 1) * half)
+                    row_info[start : start + half, 2:3] = ids_row[source, :]
+                    row_info[start : start + half, 3:4] = ids_col[source, :]
         for k in range(group // 128):
             ids = row_info[k * 128 : (k + 1) * 128, 3:4]
             col_id[:, k * 128 : (k + 1) * 128] = jnp.broadcast_to(ids, (128, 128)).T[0:8, :]
@@ -269,15 +307,17 @@
                 lab_copy(way, n + 1).wait_recv()
             if n + 2 <= (4, 3)[way]:
                 lab_copy(way, n + 2).start()
-            if n + 2 < last:
+            if n < 5:
                 ring(way, n + 2).start()
+            if n == 5:
+                ring(way, 7).start()
             sib(way, n).start()
-        if n == last - 1:
+        if n == 6:
             for o in range(1, n_z):
                 hid_copy(o).start()
         for way in range(2):
-            dist, t = RING[way][n]
-            normalize(slot_at(way, dist), 0, t)
+            _, t, slot, end = item(way, n)
+            normalize(slot, 0, t, end)
         if n == 0:
             hid_near(hidden_a).wait_recv()
             hid_local(hidden_a).wait()
@@ -285,17 +325,19 @@
         if n == 3:
             lab_near().start()
         for way in range(2):
-            dist, t = RING[way][n]
+            _, t, slot, end = item(way, n)
             sib(way, n).wait_recv()
-            normalize(slot_at(way, dist), 1, t)
-        if n % 2:
+            normalize(slot, 1, t, end)
+        if n in (1, 3, 5):
             logits_step(n // 2)
         if n == 4:
             lab_near().wait_recv()
             pair_ids()
-    logits_step(3)
-
-    row_info[:, 4:5] = 0.5 / jnp.sum(row_sum[...], axis=1, keepdims=True)
+            late_rows(core)
+        if n >= 6:
+            logits_step(n - 3)
+
+    row_info[:, 4:5] = 0.5 / row_info[:, 6:7]
     col_sum[0:1, :] = 0.5 / jnp.sum(col_sum[...], axis=0, keepdims=True)
     row_info[:, 5:6] = jnp.where(core == 0, row_info[:, 0:1], row_info[:, 1:2])
 
@@ -322,13 +364,13 @@
         return 0
 
     lax.fori_loop(0, group // chunk, chunk_step, 0)
-
+    for o in range(1, n_z):
+        hid_copy(o).wait_recv()
+    err_near(err_a).wait_recv()
+    err_local(err_a).wait()
     unpack(0, stage.at[z])
     for o in range(1, n_z):
-        hid_copy(o).wait_recv()
         unpack(SLOT_OF[o], blocks.at[SLOT_OF[o]])
-    err_near(err_a).wait_recv()
-    err_local(err_a).wait()
     total = lax.dot_general(hid[...], emb[core], TN, preferred_element_type=jnp.float32)
     for k in range(2):
         rows = slice(k * slab, (k + 1) * slab)
@@ -452,7 +494,7 @@
         right = exact(turn, right, NN) / n_rep
         q_ref[head] = right
         p_ref[head] = factor
-        new_ref[head] = memory - exact(factor, right, TN)
+        mem_ref[head] = memory
 
     finish(core, turn, full, mem[ours, :], p_own[core])
     mem_copy.wait()
@@ -505,7 +547,6 @@
             pltpu.VMEM((group, group), f32),
             pltpu.VMEM((chunk, group), jnp.bfloat16),
             pltpu.VMEM((chunk, width), f32),
-            pltpu.VMEM((group, 128), f32),
             pltpu.VMEM((8, group), f32),
             pltpu.VMEM((group, 128), f32),
             pltpu.VMEM((8, group), f32),
@@ -531,8 +572,8 @@
             pltpu.VMEM((rank, rank), f32),
             pltpu.VMEM((2, rank, slab), f32),
             pltpu.VMEM((rank, slab), f32),
-            dma((2, 7)), dma((2, 7)),
             dma((2, 8)), dma((2, 8)),
+            dma((2, 9)), dma((2, 9)),
             dma((2, 4)), dma((2, 4)),
             dma((n_z,)), dma((n_z,)),
             dma((3,)), dma((3,)),
@@ -552,16 +593,37 @@
     )(proj_a, proj_b, labels, hidden_a, hidden_b, err_a, err_b, seed)
 
 
+def update_kernel(p, q, mem, p_a, q_a, new_a, p_b, q_b, new_b):
+    for head, outs in enumerate(((p_a, q_a, new_a), (p_b, q_b, new_b))):
+        outs[0][...] = p[head]
+        outs[1][...] = q[head]
+        outs[2][0] = mem[head] - exact(p[head], q[head], TN)
+
+
+def update(p, q, mem):
+    vmem = pl.BlockSpec(memory_space=pltpu.VMEM)
+    shapes = (p.shape[1:], q.shape[1:], (1,) + mem.shape[1:]) * 2
+    return pl.pallas_call(
+        update_kernel,
+        out_shape=tuple(jax.ShapeDtypeStruct(shape, jnp.float32) for shape in shapes),
+        in_specs=[vmem] * 3,
+        out_specs=[vmem] * 6,
+        compiler_params=pltpu.CompilerParams(vmem_limit_bytes=16 * 1024 * 1024),
+        name="update",
+    )(p, q, mem)
+
+
 def shards(
     audio_hidden, score_hidden, audio_proj, score_proj, labels, q_seed, err_audio, err_score
 ):
     n_z = 8
     n_y = n_x = 4
-    p, q, new = whole(
+    p, q, mem = whole(
         n_y, n_x, n_z, audio_proj, score_proj, labels, audio_hidden, score_hidden,
         err_audio, err_score, q_seed.T,
     )
-    return (p[0].T, q[0].T, new[0:1], p[1].T, q[1].T, new[1:2])
+    p_a, q_a, new_a, p_b, q_b, new_b = update(p, q, mem)
+    return (p_a.T, q_a.T, new_a, p_b.T, q_b.T, new_b)
 
 
 def solution(mesh):

time: 132 us -> 131 us (level)
    transpose x2 -> x0, local copies, waits for them, and re-layouts: 3.34 us -> none  [shards(): return (p[0].T, q[0].T, new[0:1], p[1].T, q[1].T, new[1:2])]
    unnamed x2 -> x6, local copies, waits for them, and re-layouts: 0.01 us -> 2.96 us
    pallas_call x0 -> x1, Pallas kernels: none -> 1.64 us  [update(): pl.pallas_call(update_kernel, out_shape=tuple((jax.ShapeDtypeStruct(shape...]
    pallas_call x1, Pallas kernels: 127 us -> 125 us  [whole(): pl.pallas_call(functools.partial(whole_kernel, n_y, n_x, n_z), out_shape=...]
where the time goes in v4:
time: 131 us
  Pallas kernels  127 us (97%)
  local copies, waits for them, and re-layouts  2.96 us (2%)
    pallas_call x1, Pallas kernels, whole(): pl.pallas_call(functools.partial(whole_kernel, n_y, n_x, n_z), out_shape=...  125 us
    unnamed x6, local copies, waits for them, and re-layouts  2.96 us

profile of v4, /device:TPU:1, one launch (start us, length us, event | category | flops | bytes accessed | tf_op | source)
XLA Modules:
  0.0 130.5 jit_solution(10197939434287998483)
XLA Ops:
  0.6 125.3 %whole.1 = (f32[2,64,80]{2,1,0:T(8,128)}, f32[2,64,1024]{2,1,0:T(8,128)}, f32[2,80,1024]{2,1,0:T(8,128)}) custom-call(bf16[160,1024]{1,0:T(8,128)(2,1)} %proj_a.1, bf16[160,1024]{1,0:T(8,128)(2,1)} %proj_b.1, s32[1,160]{1,0:T(1,128)} %labels.1, bf16[160,1280]{1,0:T(8,128)(2,1)} %hidden_a.1, bf16[160,1280]{1,0:T(8,128)(2,1)} %hidden_b.1, ...), custom_call_target="tpu_custom_call" | custom-call | tf_op jit(solution)/shard_map/whole/pallas_call | solution.py:535
  125.9 0.0 copy-start
  125.9 1.1 copy-done
  127.0 0.0 copy-start.1
  127.0 1.0 copy-done.1
  128.1 0.0 copy-start.2
  128.1 0.8 copy-done.2
  128.9 1.6 %update.1 = (f32[64,80]{1,0:T(8,128)}, f32[64,1024]{1,0:T(8,128)}, f32[1,80,1024]{2,1,0:T(8,128)}, f32[64,80]{1,0:T(8,128)}, f32[64,1024]{1,0:T(8,128)}, /*index=5*/f32[1,80,1024]{2,1,0:T(8,128)}) custom-call(f32[2,64,80]{2,1,0:T(8,128)S(1)} %copy-done.2, f32[2,64,1024]{2,1,0:T(8,128)S(1)} %copy-done.1, f32[2,80,1024]{2,1,0:T(8,128)S(1)} %copy-done), custom_call_target="tpu_custom_call" | custom-call | tf_op jit(solution)/shard_map/update/pallas_call | solution.py:606
Async XLA Ops:
  125.9 1.1 copy-start
  127.0 1.0 copy-start.1
  128.1 0.8 copy-start.2

commit v5 on v4

--- a/solution.py
+++ b/solution.py
@@ -242,11 +242,9 @@
         else:
             for k in range(new_rows // rows):
                 tile_logits(k * rows, rows, old_cols, cols)
-        if step == 2:
-            late_rows(other)
-        elif step == 1:
+        if step == 1:
             lax.fori_loop(0, old_cols // COL_TILE[step], more, 0)
-        elif old_cols:
+        elif step > 2:
             for k in range(old_cols // COL_TILE[step]):
                 tile_logits(old_rows, new_rows - old_rows, k * COL_TILE[step], COL_TILE[step])
 
@@ -300,7 +298,8 @@
             col_id[:, k * 128 : (k + 1) * 128] = jnp.broadcast_to(ids, (128, 128)).T[0:8, :]
 
     last = len(RING[0])
-    for n in range(last):
+
+    def forward(n):
         for way in range(2):
             ring(way, n).wait_recv()
             if n < (4, 3)[way]:
@@ -312,30 +311,42 @@
             if n == 5:
                 ring(way, 7).start()
             sib(way, n).start()
-        if n == 6:
-            for o in range(1, n_z):
-                hid_copy(o).start()
+
+    def arrived(n, cross):
         for way in range(2):
             _, t, slot, end = item(way, n)
-            normalize(slot, 0, t, end)
+            if cross:
+                sib(way, n).wait_recv()
+            normalize(slot, cross, t, end)
+
+    for n in range(6):
+        forward(n)
+        arrived(n, 0)
         if n == 0:
             hid_near(hidden_a).wait_recv()
             hid_local(hidden_a).wait()
             pack()
         if n == 3:
             lab_near().start()
-        for way in range(2):
-            _, t, slot, end = item(way, n)
-            sib(way, n).wait_recv()
-            normalize(slot, 1, t, end)
-        if n in (1, 3, 5):
+        arrived(n, 1)
+        if n in (1, 3):
             logits_step(n // 2)
         if n == 4:
             lab_near().wait_recv()
             pair_ids()
             late_rows(core)
-        if n >= 6:
-            logits_step(n - 3)
+    late_rows(other)
+    forward(6)
+    for o in range(1, n_z):
+        hid_copy(o).start()
+    arrived(6, 0)
+    logits_step(2)
+    forward(7)
+    arrived(7, 0)
+    arrived(6, 1)
+    logits_step(3)
+    arrived(7, 1)
+    logits_step(4)
 
     row_info[:, 4:5] = 0.5 / row_info[:, 6:7]
     col_sum[0:1, :] = 0.5 / jnp.sum(col_sum[...], axis=0, keepdims=True)
@@ -412,11 +423,6 @@
     tail = [packed[rank:, g * 32 : (g + 1) * 32] for g in range(4)]
     left = jnp.concatenate([packed[:rank, :], jnp.concatenate(tail, axis=0)], axis=1)
 
-    gram = exact(left, left, NT)
-    gram_sum = all_sum(
-        g_buf, z, n_z, g_send, g_recv, plane,
-        jnp.concatenate([gram[: rank // 2, :], gram[rank // 2 :, :]], axis=1),
-    )
     right = exact(left, mem[...], NN)
     span = width // 2
     for k in range(n_rep):
@@ -431,6 +437,19 @@
     ]
     for one in reduce:
         one.start()
+
+    gram = exact(left, left, NT)
+    gram_sum = all_sum(
+        g_buf, z, n_z, g_send, g_recv, plane,
+        jnp.concatenate([gram[: rank // 2, :], gram[rank // 2 :, :]], axis=1),
+    )
+
+    for one in reduce:
+        one.wait()
+    total = gathered[0]
+    for k in range(1, n_rep):
+        total = total + gathered[k]
+    z_sum = all_sum(z_buf, z, n_z, z_send, z_recv, plane, total)
 
     gram = gram_sum()
     resid[...] = jnp.concatenate([gram[:, :rank], gram[:, rank:]], axis=0)
@@ -452,15 +471,7 @@
         resid[...] = values - column * (w * inverse)
         return 0
 
-    cuts = [0, rank // 3, 2 * rank // 3, rank]
-    lax.fori_loop(cuts[0], cuts[1], column_step, 0)
-    for one in reduce:
-        one.wait()
-    total = gathered[0]
-    for k in range(1, n_rep):
-        total = total + gathered[k]
-    z_sum = all_sum(z_buf, z, n_z, z_send, z_recv, plane, total)
-    lax.fori_loop(cuts[1], cuts[2], column_step, 0)
+    lax.fori_loop(0, rank // 2, column_step, 0)
     full[rep] = z_sum()
     spread = [
         remote(full.at[rep], full.at[rep], f_send.at[i], f_recv.at[i], along_rep(i))
@@ -468,7 +479,7 @@
     ]
     for one in spread:
         one.start()
-    lax.fori_loop(cuts[2], cuts[3], column_step, 0)
+    lax.fori_loop(rank // 2, rank, column_step, 0)
 
     turn_copy = remote(basis, basis_sib, pair_send.at[2], pair_recv.at[2], sibling)
     turn_copy.start()
@@ -608,7 +619,7 @@
         out_shape=tuple(jax.ShapeDtypeStruct(shape, jnp.float32) for shape in shapes),
         in_specs=[vmem] * 3,
         out_specs=[vmem] * 6,
-        compiler_params=pltpu.CompilerParams(vmem_limit_bytes=16 * 1024 * 1024),
+        compiler_params=pltpu.CompilerParams(vmem_limit_bytes=60 * 1024 * 1024),
         name="update",
     )(p, q, mem)
 

time: 131 us -> 128 us (0.977)
  local copies, waits for them, and re-layouts: 2.96 us -> 0 us
    unnamed x6 -> x0, local copies, waits for them, and re-layouts: 2.96 us -> none
where the time goes in v5:
time: 128 us
  Pallas kernels  127 us (99%)
    pallas_call x1, Pallas kernels, whole(): pl.pallas_call(functools.partial(whole_kernel, n_y, n_x, n_z), out_shape=...  125 us
    pallas_call x1, Pallas kernels, update(): pl.pallas_call(update_kernel, out_shape=tuple((jax.ShapeDtypeStruct(shape...  2.9 us

profile of v5, /device:TPU:1, one launch (start us, length us, event | category | flops | bytes accessed | tf_op | source)
XLA Modules:
  0.0 128.1 jit_solution(11765305414364426416)
XLA Ops:
  0.6 124.5 %whole.1 = (f32[2,64,80]{2,1,0:T(8,128)}, f32[2,64,1024]{2,1,0:T(8,128)}, f32[2,80,1024]{2,1,0:T(8,128)}) custom-call(bf16[160,1024]{1,0:T(8,128)(2,1)} %proj_a.1, bf16[160,1024]{1,0:T(8,128)(2,1)} %proj_b.1, s32[1,160]{1,0:T(1,128)} %labels.1, bf16[160,1280]{1,0:T(8,128)(2,1)} %hidden_a.1, bf16[160,1280]{1,0:T(8,128)(2,1)} %hidden_b.1, ...), custom_call_target="tpu_custom_call" | custom-call | tf_op jit(solution)/shard_map/whole/pallas_call | solution.py:546
  125.2 2.9 %update.1 = (f32[64,80]{1,0:T(8,128)}, f32[64,1024]{1,0:T(8,128)}, f32[1,80,1024]{2,1,0:T(8,128)}, f32[64,80]{1,0:T(8,128)}, f32[64,1024]{1,0:T(8,128)}, /*index=5*/f32[1,80,1024]{2,1,0:T(8,128)}) custom-call(f32[2,64,80]{2,1,0:T(8,128)} %get-tuple-element.15.p, f32[2,64,1024]{2,1,0:T(8,128)} %get-tuple-element.16.q, f32[2,80,1024]{2,1,0:T(8,128)} %get-tuple-element.17.mem), custom_call_target="tpu_custom_call" | custom-call | tf_op jit(solution)/shard_map/update/pallas_call | solution.py:617

commit v6 on v5

--- a/solution.py
+++ b/solution.py
@@ -418,8 +418,18 @@
         + [jnp.concatenate([left[g * strip : (g + 1) * strip, 128:] for g in range(4)], axis=1)],
         axis=0,
     )
-    packed = all_sum(x_buf, x, n_x, x_send, x_recv, along_x, packed)()
-    packed = all_sum(y_buf, y, n_y, y_send, y_recv, along_y, packed)()
+    middle = packed.shape[0] // 2
+
+    def over_x(k, value):
+        return all_sum(x_buf.at[k], x, n_x, x_send.at[k], x_recv.at[k], along_x, value)
+
+    def over_y(k, value):
+        return all_sum(y_buf.at[k], y, n_y, y_send.at[k], y_recv.at[k], along_y, value)
+
+    top, low = over_x(0, packed[:middle]), over_y(1, packed[middle:])
+    top = over_y(0, top())
+    low = over_x(1, low())
+    packed = jnp.concatenate([top(), low()], axis=0)
     tail = [packed[rank:, g * 32 : (g + 1) * 32] for g in range(4)]
     left = jnp.concatenate([packed[:rank, :], jnp.concatenate(tail, axis=0)], axis=1)
 
@@ -569,8 +579,8 @@
             pltpu.VMEM((2, slab, width), f32),
             pltpu.VMEM((feat, width), f32),
             pltpu.VMEM((slab, width), f32),
-            pltpu.VMEM((n_x, slab, 2 * rank), f32),
-            pltpu.VMEM((n_y, slab, 2 * rank), f32),
+            pltpu.VMEM((2, n_x, slab // 2, 2 * rank), f32),
+            pltpu.VMEM((2, n_y, slab // 2, 2 * rank), f32),
             pltpu.VMEM((n_z, rank // 2, 2 * rank), f32),
             pltpu.VMEM((n_rep, 8, width // 2), f32),
             pltpu.VMEM((n_rep, 8, width // 2), f32),
@@ -589,8 +599,8 @@
             dma((n_z,)), dma((n_z,)),
             dma((3,)), dma((3,)),
             dma((4,)),
-            dma((n_x,)), dma((n_x,)),
-            dma((n_y,)), dma((n_y,)),
+            dma((2, n_x)), dma((2, n_x)),
+            dma((2, n_y)), dma((2, n_y)),
             dma((n_z,)), dma((n_z,)),
             dma((n_rep,)), dma((n_rep,)),
             dma((n_z,)), dma((n_z,)),

time: 128 us -> 127 us (level)
  no operation moved by 1% of the time
where the time goes in v6:
time: 127 us
  Pallas kernels  127 us (100%)
    pallas_call x1, Pallas kernels, whole(): pl.pallas_call(functools.partial(whole_kernel, n_y, n_x, n_z), out_shape=...  124 us
    pallas_call x1, Pallas kernels, update(): pl.pallas_call(update_kernel, out_shape=tuple((jax.ShapeDtypeStruct(shape...  2.9 us

profile of v6, /device:TPU:1, one launch (start us, length us, event | category | flops | bytes accessed | tf_op | source)
XLA Modules:
  0.0 127.4 jit_solution(3259188357643093284)
XLA Ops:
  0.6 123.8 %whole.1 = (f32[2,64,80]{2,1,0:T(8,128)}, f32[2,64,1024]{2,1,0:T(8,128)}, f32[2,80,1024]{2,1,0:T(8,128)}) custom-call(bf16[160,1024]{1,0:T(8,128)(2,1)} %proj_a.1, bf16[160,1024]{1,0:T(8,128)(2,1)} %proj_b.1, s32[1,160]{1,0:T(1,128)} %labels.1, bf16[160,1280]{1,0:T(8,128)(2,1)} %hidden_a.1, bf16[160,1280]{1,0:T(8,128)(2,1)} %hidden_b.1, ...), custom_call_target="tpu_custom_call" | custom-call | tf_op jit(solution)/shard_map/whole/pallas_call | solution.py:556
  124.5 2.9 %update.1 = (f32[64,80]{1,0:T(8,128)}, f32[64,1024]{1,0:T(8,128)}, f32[1,80,1024]{2,1,0:T(8,128)}, f32[64,80]{1,0:T(8,128)}, f32[64,1024]{1,0:T(8,128)}, /*index=5*/f32[1,80,1024]{2,1,0:T(8,128)}) custom-call(f32[2,64,80]{2,1,0:T(8,128)} %get-tuple-element.15.p, f32[2,64,1024]{2,1,0:T(8,128)} %get-tuple-element.16.q, f32[2,80,1024]{2,1,0:T(8,128)} %get-tuple-element.17.mem), custom_call_target="tpu_custom_call" | custom-call | tf_op jit(solution)/shard_map/update/pallas_call | solution.py:627
